TPU v7x, 128 devices: a whole 4x4x4 slice. The times are simulated.
128 devices in a mesh: section: 4 (over x_lo, core), fsdp: 32 (over x_hi, z, y).
Axes of the slice: x: 4 (x_hi: 2, x_lo: 2; x = x_hi * 2 + x_lo), y: 4, z: 4, core: 2. Of those that a mesh axis runs over, the one named last changes fastest.
Arguments:
- saved_inputs: bfloat16 [4, 2, 32, 512, 1536], P('section', None, 'fsdp'), may hold values from -6 to 6
- grad_outputs: bfloat16 [2, 32, 512, 1536], P(None, 'fsdp'), may hold values from -6 to 6
- lengths: int32 [2, 32], P(None, 'fsdp'), may hold values from 256 to 512, as said below
- pointwise: bfloat16 [4, 1536, 1536], P('section', 'fsdp'), may hold values from -0.15625 to 0.15625
- depth_kernel: bfloat16 [4, 5, 1536], P('section', None, 'fsdp'), may hold values from -2.5 to 2.5
- norm_gain: bfloat16 [4, 1536], P('section', 'fsdp'), may hold values from 0.5 to 1.5
Outputs:
- frame_grads: bfloat16 [4, 2, 32, 512, 1536], P('section', None, 'fsdp')
- pointwise_grad: float32 [4, 1536, 1536], P('section', 'fsdp')
- kernel_grad: float32 [4, 5, 1536], P('section', None, 'fsdp')
- gain_grad: float32 [4, 1536], P('section', 'fsdp')
Inputs may be any that keep to these rules, and one draw needn't show every extreme that they name: `lengths`: frames at and after an utterance's length are padding; some utterance fills all 512 slots.
All inputs are finite; a program needn't handle non-finite values.
Results may differ from a plain program's by a relative error of at most 0.0057.
Values may be sent and summed in bfloat16 or wider, within the bound.
No kernel may reach another device: no remote copies, remote signals or barrier semaphores. Data moves between devices by JAX's collectives and lax.ppermute only.
A program may use at most 128 MiB of HBM per device.

v0:
```python
import functools

import jax
import jax.numpy as jnp
import numpy as np
from jax import lax
from jax.experimental import pallas as pl
from jax.experimental.pallas import tpu as pltpu
from jax.sharding import Mesh
from jax.sharding import PartitionSpec as P

EPSILON = 1e-05
F32 = jnp.float32
BF16 = jnp.bfloat16
LANES = 128
PAD = 8
ANY = pl.BlockSpec(memory_space=pl.ANY)
HBM = pl.BlockSpec(memory_space=pltpu.HBM)
SMEM = pl.BlockSpec(memory_space=pltpu.SMEM)
VMEM = pl.BlockSpec(memory_space=pltpu.VMEM)

def params(limit, **kw):
    return pltpu.CompilerParams(vmem_limit_bytes=limit << 20, **kw)


def cost(us):
    return pl.CostEstimate(flops=int(us * 1.0e9), bytes_accessed=1 << 20, transcendentals=0)


def partners(core):
    near, mirrored = [i ^ 1 for i in range(4)], [3 - i for i in range(4)]
    return (near, mirrored) if core == 0 else (mirrored, near)


def tables():
    gather = np.zeros((2, 2, 4, 4, 2, 4, 4, 2), np.int32)
    scatter = np.zeros((2, 2, 4, 4, 2, 32), np.int32)
    for core, x, z, y, half in np.ndindex(2, 2, 4, 4, 2):
        inner, outer = (y, z) if half == 0 else (z, y)
        one, two = partners(core)

        def block(a, b, r):
            zz, yy = (a, b) if half == 0 else (b, a)
            return (x + r) % 2 * 16 + zz * 4 + yy

        def order(me):
            return me, one[me], two[me], one[two[me]]

        for o, a in enumerate(order(outer)):
            for i, b in enumerate(order(inner)):
                for r in range(2):
                    gather[core, x, z, y, half, o, i, r] = block(a, b, r)
                    at = (3, 1, 2, 0)
                    place = at.index(o) * 8 + at.index(i) * 2 + r
                    scatter[core, x, z, y, half, block(a, b, r)] = place
    return np.concatenate([gather.reshape(64, -1), scatter.reshape(64, -1)], axis=-1)


def forward_kernel(m, lens, x_in, taps, normed_out, slope_out, inv_out, act_out, *rest):
    x_ref, hid, mix, normed_ref, slope_ref, inv_ref, act, act_ref, sem, sems = rest
    length = lens[m]
    frames, feats = x_ref.shape
    cols = feats // LANES
    copy = pltpu.make_async_copy(x_in.at[m], x_ref, sem)
    copy.start()
    for c in range(cols):
        hid[c, 0:PAD, :] = jnp.zeros((PAD, LANES), F32)
        hid[c, PAD + frames : 2 * PAD + frames, :] = jnp.zeros((PAD, LANES), F32)
    copy.wait()

    def load(i, carry):
        r = pl.multiple_of(i * 16, 16)
        rows = r + lax.broadcasted_iota(jnp.int32, (16, LANES), 0)
        keep = rows < length
        for c in range(cols):
            v = x_ref[pl.ds(r, 16), c * LANES : (c + 1) * LANES].astype(F32)
            hid[c, pl.ds(r + PAD, 16), :] = jnp.where(keep, v, 0.0)
        return carry

    lax.fori_loop(0, frames // 16, load, 0, unroll=2)

    def conv(i, carry):
        r = pl.multiple_of(i * 64, 64)
        for c in range(cols):
            span = slice(c * LANES, (c + 1) * LANES)
            total = taps[0:1, span] * hid[c, pl.ds(r + PAD - 2, 64), :]
            for k in range(1, 5):
                total = total + taps[k : k + 1, span] * hid[c, pl.ds(r + PAD - 2 + k, 64), :]
            mix[pl.ds(r, 64), span] = total
        return carry

    lax.fori_loop(0, frames // 64, conv, 0)

    def norm(i, carry):
        r = pl.multiple_of(i * 16, 16)
        keep = r + lax.broadcasted_iota(jnp.int32, (16, 1), 0) < length
        mixed = mix[pl.ds(r, 16), :]
        centred = mixed - jnp.mean(mixed, axis=-1, keepdims=True)
        inverse = lax.rsqrt(jnp.mean(centred * centred, axis=-1, keepdims=True) + EPSILON)
        gain = taps[5:6, :]
        normed = centred * inverse
        gained = normed * gain
        logistic = jax.nn.sigmoid(gained)
        normed_ref[pl.ds(r, 16), :] = normed.astype(BF16)
        slope = (logistic + gained * logistic * (1.0 - logistic)) * gain
        slope_ref[pl.ds(r, 16), :] = jnp.where(keep, slope, 0.0).astype(BF16)
        act[pl.ds(r, 16), :] = jnp.where(keep, gained * logistic, 0.0).astype(BF16)
        inv_ref[pl.ds(r, 16), :] = jnp.broadcast_to(inverse, (16, LANES))
        return carry

    outs = ((normed_ref, normed_out), (slope_ref, slope_out), (inv_ref, inv_out))

    def quarter(q, carry):
        lax.fori_loop(0, frames // 64, lambda i, c: norm(q * (frames // 64) + i, c), 0, unroll=2)
        part = pl.ds(pl.multiple_of(q * (frames // 4), frames // 4), frames // 4)
        for n, (held, out) in enumerate(outs):
            pltpu.make_async_copy(held.at[part], out.at[part], sems.at[n]).start()
        return carry

    lax.fori_loop(0, 4, quarter, 0)
    for c in range(feats // 256):
        span = slice(c * 256, (c + 1) * 256)
        act_ref[span, :] = act[:, span].T
        pltpu.make_async_copy(act_ref.at[span], act_out.at[span], sems.at[3]).start()
    for n, (held, out) in enumerate(outs + ((act_ref, act_out),)):
        pltpu.make_async_copy(held, out, sems.at[n]).wait()


def forward(m, lens, x, taps):
    micro, frames, feats = x.shape
    return pl.pallas_call(
        functools.partial(forward_kernel, m),
        in_specs=[SMEM, HBM, VMEM],
        out_specs=[HBM] * 4,
        out_shape=[
            jax.ShapeDtypeStruct((frames, feats), BF16),
            jax.ShapeDtypeStruct((frames, feats), BF16),
            jax.ShapeDtypeStruct((frames, LANES), F32),
            jax.ShapeDtypeStruct((feats, frames), BF16),
        ],
        scratch_shapes=[
            pltpu.VMEM((frames, feats), BF16),
            pltpu.VMEM((feats // LANES, frames + 2 * PAD, LANES), F32),
            pltpu.VMEM((frames, feats), F32),
            pltpu.VMEM((frames, feats), BF16),
            pltpu.VMEM((frames, feats), BF16),
            pltpu.VMEM((frames, LANES), F32),
            pltpu.VMEM((frames, feats), BF16),
            pltpu.VMEM((feats, frames), BF16),
            pltpu.SemaphoreType.DMA,
            pltpu.SemaphoreType.DMA((4,)),
        ],
        compiler_params=params(60),
        cost_estimate=cost(8),
    )(lens, x, taps)


def relay_kernel(first, who, meta, grads, come, come_one, *rest):
    (wa, wb), rest = (rest[:2], rest[2:4]), rest[4:]
    (normed_in, slope_in, inv_in), taps, rest = (rest[0:2], rest[2:4], rest[4:6]), rest[6], rest[7:]
    if not first:
        rest = rest[2:]
    send, mixed_out, gain_out = rest[:3]
    w, up, normed, slope, inv, ga, gmix, narrow, out, gsum, low, high, sems = rest[3:]
    frames, feats = up.shape
    cols = feats // LANES
    half = feats // 2
    rows = 48
    section, place_x = meta[0], meta[3]
    turn = sum(jnp.where(section == i, m, 0) for i, m in enumerate(who))
    active, slot = turn >= 0, jnp.maximum(turn, 0)
    last, length = section == 3, meta[1 + slot]

    def pieces(group):
        made = []
        odd = (place_x + group) % 2
        for h, parts in enumerate((wa, wb)):
            for p in range(2):
                for j in range(8):
                    at = h * 32 + p * 16 + 2 * j + odd
                    place = pl.multiple_of(meta[8 + at] * rows, 16)
                    made.append(
                        pltpu.make_async_copy(
                            parts[p].at[2 * j + odd],
                            w.at[pl.ds(place, rows), pl.ds(h * half, half)],
                            sems.at[0 if group == 0 else 8],
                        )
                    )
        return made

    @pl.when(active)
    def _():
        @pl.when(last)
        def _():
            pltpu.make_async_copy(grads.at[slot], up, sems.at[1]).start()

        @pl.when(section == 1)
        def _():
            pltpu.make_async_copy(come_one, up, sems.at[1]).start()

        @pl.when(jnp.logical_and(section != 3, section != 1))
        def _():
            pltpu.make_async_copy(come, up, sems.at[1]).start()

        weights = [pieces(0), pieces(1)]
        for copy in weights[0]:
            copy.start()
        for m in range(2):

            @pl.when(slot == m)
            def _():
                pltpu.make_async_copy(slope_in[m], slope, sems.at[3]).start()
                pltpu.make_async_copy(normed_in[m], normed, sems.at[2]).start()
                pltpu.make_async_copy(inv_in[m], inv, sems.at[4]).start()

        for copy in weights[1]:
            copy.start()
        for c in range(cols):
            gmix[c, 0:PAD, :] = jnp.zeros((PAD, LANES), F32)
            gmix[c, PAD + frames : 2 * PAD + frames, :] = jnp.zeros((PAD, LANES), F32)
        low[...] = jnp.zeros_like(low)
        high[...] = jnp.zeros_like(high)

        def multiply(n):
            ga[:, n * 256 : (n + 1) * 256] = lax.dot_general(
                up[...],
                w[n * 256 : (n + 1) * 256, :],
                (((1,), (1,)), ((), ())),
                preferred_element_type=F32,
            )

        def weigh(n):
            span = slice(n * 256, (n + 1) * 256)
            total = jnp.zeros((8, 256), F32)
            for r in range(0, frames, 32):
                part = slice(r, r + 32)
                gn = ga[part, span] * slope[part, span].astype(F32)
                both = gn * normed[part, span].astype(F32)
                ga[part, span] = gn
                low[part, :] += gn[:, :LANES] + gn[:, LANES:]
                high[part, :] += both[:, :LANES] + both[:, LANES:]
                total = total + (both[:8] + both[8:16]) + (both[16:24] + both[24:])
            gsum[:, span] = total

        pltpu.make_async_copy(come, up, sems.at[1]).wait()
        for copy in weights[0]:
            copy.wait()
        multiply(0)
        pltpu.make_async_copy(slope_in[0], slope, sems.at[3]).wait()
        pltpu.make_async_copy(normed_in[0], normed, sems.at[2]).wait()
        pltpu.make_async_copy(inv_in[0], inv, sems.at[4]).wait()
        count = feats // 256
        for n in range(1, count):
            if n == count // 2:
                for copy in weights[1]:
                    copy.wait()
            multiply(n)
            weigh(n - 1)
        weigh(count - 1)
        gain_copy = pltpu.make_async_copy(gsum, gain_out.at[slot], sems.at[6])
        gain_copy.start()

        def means(i, carry):
            r = pl.multiple_of(i * 64, 64)
            for ref in (low, high):
                mean = jnp.sum(ref[pl.ds(r, 64), :], axis=-1, keepdims=True) * (1.0 / feats)
                ref[pl.ds(r, 64), :] = jnp.broadcast_to(mean, (64, LANES))
            return carry

        lax.fori_loop(0, frames // 64, means, 0, unroll=2)

        def finish(i, carry):
            r = pl.multiple_of(i * 16, 16)
            a, b, scale = low[pl.ds(r, 16), :], high[pl.ds(r, 16), :], inv[pl.ds(r, 16), :]
            for c in range(cols):
                span = slice(c * LANES, (c + 1) * LANES)
                nm = normed[pl.ds(r, 16), span].astype(F32)
                mixed = scale * (ga[pl.ds(r, 16), span] - a - nm * b)
                narrow[pl.ds(r, 16), span] = mixed.astype(BF16)
                gmix[c, pl.ds(r + PAD, 16), :] = mixed
            return carry

        lax.fori_loop(0, frames // 16, finish, 0, unroll=2)
        saved = pltpu.make_async_copy(narrow, mixed_out.at[slot], sems.at[5])
        saved.start()

        def conv(i, carry):
            r = pl.multiple_of(i * 64, 64)
            keep = r + lax.broadcasted_iota(jnp.int32, (64, LANES), 0) < length
            for c in range(cols):
                span = slice(c * LANES, (c + 1) * LANES)
                total = taps[4:5, span] * gmix[c, pl.ds(r + PAD - 2, 64), :]
                for k in range(1, 5):
                    total = total + taps[4 - k : 5 - k, span] * gmix[c, pl.ds(r + PAD - 2 + k, 64), :]
                result = up[pl.ds(r, 64), span].astype(F32) + jnp.where(keep, total, 0.0)
                out[pl.ds(r, 64), span] = result.astype(BF16)
            part = pl.ds(r, 64)
            pltpu.make_async_copy(out.at[part], send.at[part], sems.at[7]).start()
            return carry

        lax.fori_loop(0, frames // 64, conv, 0)
        pltpu.make_async_copy(out, send, sems.at[7]).wait()
        saved.wait()
        gain_copy.wait()


def relay(who, meta, grads, come, come_one, weights, saved, taps, state):
    micro, frames, feats = grads.shape
    cols = feats // LANES
    first = state is None
    shapes = [
        jax.ShapeDtypeStruct((frames, feats), BF16),
        jax.ShapeDtypeStruct((micro, frames, feats), BF16),
        jax.ShapeDtypeStruct((micro, 8, feats), F32),
    ]
    operands = [meta, grads, come, come_one, *weights, *saved, taps]
    specs = [SMEM, HBM, ANY, ANY] + [HBM] * (len(operands) - 5) + [VMEM]
    aliases = {}
    if not first:
        aliases = {len(operands) + i: 1 + i for i in range(2)}
        operands += list(state)
        specs += [HBM] * 2
    out = pl.pallas_call(
        functools.partial(relay_kernel, first, who),
        in_specs=specs,
        out_specs=[ANY] + [HBM] * 2,
        out_shape=shapes,
        input_output_aliases=aliases,
        scratch_shapes=[
            pltpu.VMEM((feats, feats), BF16),
            pltpu.VMEM((frames, feats), BF16),
            pltpu.VMEM((frames, feats), BF16),
            pltpu.VMEM((frames, feats), BF16),
            pltpu.VMEM((frames, LANES), F32),
            pltpu.VMEM((frames, feats), F32),
            pltpu.VMEM((cols, frames + 2 * PAD, LANES), F32),
            pltpu.VMEM((frames, feats), BF16),
            pltpu.VMEM((frames, feats), BF16),
            pltpu.VMEM((8, feats), F32),
            pltpu.VMEM((frames, LANES), F32),
            pltpu.VMEM((frames, LANES), F32),
            pltpu.SemaphoreType.DMA((10,)),
        ],
        compiler_params=params(60),
        cost_estimate=cost(1),
    )(*operands)
    return out[0], tuple(out[1:])


def weight_kernel(meta, act_a, act_b, *rest):
    sources, outs, (act, gm, acc, block, sems) = rest[:7], rest[7:11], rest[11:]
    feats, frames = act_a.shape
    half = feats // 2
    section = meta[0]
    copies = [
        pltpu.make_async_copy(act_a, act.at[:, pl.ds(0, frames)], sems.at[0]),
        pltpu.make_async_copy(act_b, act.at[:, pl.ds(frames, frames)], sems.at[1]),
    ]
    for copy in copies:
        copy.start()
    for m in range(2):
        for owner in range(4):

            @pl.when(section == owner)
            def _():
                source = sources[0].at[m] if owner == 3 else sources[1 + 2 * owner + m]
                place = gm.at[pl.ds(m * frames, frames)]
                pltpu.make_async_copy(source, place, sems.at[2 + m]).start()

    for m in range(2):
        copies[m].wait()
        pltpu.make_async_copy(sources[1], gm.at[pl.ds(m * frames, frames)], sems.at[2 + m]).wait()
    leaving = []
    rows = 48
    for h in range(2):

        def multiply(n, carry):
            r = pl.multiple_of(n * 384, 384)
            acc[...] = lax.dot_general(
                act[pl.ds(r, 384), :],
                gm[:, h * half : (h + 1) * half],
                (((1,), (0,)), ((), ())),
                preferred_element_type=F32,
            )
            for q in range(8):
                place = meta[72 + h * 32 + n * 8 + q]
                block[h, place] = acc[q * rows : (q + 1) * rows, :].astype(BF16)
            return carry

        lax.fori_loop(0, feats // 384, multiply, 0)
        for p in range(2):
            copy = pltpu.make_async_copy(
                block.at[h, pl.ds(p * 16, 16)], outs[h * 2 + p], sems.at[4 + h * 2 + p]
            )
            copy.start()
            leaving.append(copy)
    for copy in leaving:
        copy.wait()


def weight_terms(meta, acts, grads, comes):
    feats, frames = acts[0].shape
    half = feats // 2
    operands = [meta, *acts, grads, *comes]
    return pl.pallas_call(
        weight_kernel,
        in_specs=[SMEM, ANY, ANY, HBM] + [ANY] * len(comes),
        out_specs=[ANY] * 4,
        out_shape=[jax.ShapeDtypeStruct((16, 48, half), BF16)] * 4,
        scratch_shapes=[
            pltpu.VMEM((feats, 2 * frames), BF16),
            pltpu.VMEM((2 * frames, feats), BF16),
            pltpu.VMEM((384, half), F32),
            pltpu.VMEM((2, 32, 48, half), BF16),
            pltpu.SemaphoreType.DMA((12,)),
        ],
        compiler_params=params(60),
        cost_estimate=cost(8),
    )(*operands)


def tap_kernel(m, meta, x_in, mixed_in, gain_in, taps, *rest):
    count = 6 if m == 1 else 0
    sent, rest = rest[:count], rest[count:]
    if count:
        out, frame_out, x_ref, mixed_ref, gain_ref, hid, sems, held, more = rest
    else:
        out, x_ref, mixed_ref, gain_ref, hid, sems = rest
    section = meta[0]
    length = meta[1 + m]
    frames, feats = x_ref.shape
    cols = feats // LANES
    copies = [
        pltpu.make_async_copy(x_in.at[m], x_ref, sems.at[0]),
        pltpu.make_async_copy(mixed_in.at[m], mixed_ref, sems.at[1]),
        pltpu.make_async_copy(gain_in.at[m], gain_ref, sems.at[2]),
    ]
    for copy in copies:
        copy.start()
    if count:
        for owner, turns in enumerate(((4, 5), (3, 4), (1, 2), (0, 1))):

            @pl.when(section == owner)
            def _():
                for p in range(2):
                    pltpu.make_async_copy(sent[turns[p]], held.at[p], more.at[p]).start()

    for c in range(cols):
        hid[c, 0:PAD, :] = jnp.zeros((PAD, LANES), F32)
        hid[c, PAD + frames : 2 * PAD + frames, :] = jnp.zeros((PAD, LANES), F32)
    copies[0].wait()

    def load(i, carry):
        r = pl.multiple_of(i * 16, 16)
        keep = r + lax.broadcasted_iota(jnp.int32, (16, LANES), 0) < length
        for c in range(cols):
            v = x_ref[pl.ds(r, 16), c * LANES : (c + 1) * LANES].astype(F32)
            hid[c, pl.ds(r + PAD, 16), :] = jnp.where(keep, v, 0.0)
        return carry

    lax.fori_loop(0, frames // 16, load, 0, unroll=2)
    copies[1].wait()
    copies[2].wait()
    leave = None
    if count:
        for p in range(2):
            pltpu.make_async_copy(sent[0], held.at[p], more.at[p]).wait()
        leave = pltpu.make_async_copy(held, frame_out, more.at[2])
        leave.start()
    for c in range(cols):
        span = slice(c * LANES, (c + 1) * LANES)

        def add(i, sums):
            r = pl.multiple_of(i * 32, 32)
            grown = list(sums)
            wide = mixed_ref[pl.ds(r, 32), span].astype(F32)
            for q in range(4):
                g = wide[8 * q : 8 * q + 8]
                for k in range(5):
                    grown[k] = grown[k] + g * hid[c, pl.ds(r + PAD - 2 + k + 8 * q, 8), :]
            return tuple(grown)

        sums = lax.fori_loop(0, frames // 32, add, (jnp.zeros((8, LANES), F32),) * 5, unroll=2)
        for k in range(5):
            out[k : k + 1, span] = jnp.sum(sums[k], axis=0, keepdims=True)
    out[5:6, :] = jnp.sum(gain_ref[...], axis=0, keepdims=True) / taps[5:6, :]
    out[6:8, :] = jnp.zeros((2, feats), F32)
    if count:
        leave.wait()


def tap_terms(m, meta, x, mixed, gain, taps, sent):
    micro, frames, feats = x.shape
    more = len(sent) > 0
    made = pl.pallas_call(
        functools.partial(tap_kernel, m),
        in_specs=[SMEM, HBM, HBM, HBM, VMEM] + [HBM] * len(sent),
        out_specs=[VMEM] + [HBM] * more,
        out_shape=[jax.ShapeDtypeStruct((8, feats), F32)]
        + [jax.ShapeDtypeStruct(x.shape, BF16)] * more,
        scratch_shapes=[
            pltpu.VMEM((frames, feats), BF16),
            pltpu.VMEM((frames, feats), BF16),
            pltpu.VMEM((8, feats), F32),
            pltpu.VMEM((feats // LANES, frames + 2 * PAD, LANES), F32),
            pltpu.SemaphoreType.DMA((3,)),
        ]
        + [pltpu.VMEM(x.shape, BF16), pltpu.SemaphoreType.DMA((3,))] * more,
        compiler_params=params(60),
        cost_estimate=cost(5),
    )(meta, x, mixed, gain, taps, *sent)
    return made[0], (made[1] if more else None)


def swap(x, axis, d):
    n = lax.axis_size(axis)
    return lax.ppermute(x, axis, [(i, i ^ d) for i in range(n)])


def meet(x, axis, step):
    n = lax.axis_size(axis)
    route = [
        (s * n + i, s * n + partners(s % 2)[step][i])
        for s in range(lax.axis_size("section"))
        for i in range(n)
    ]
    return lax.ppermute(x, ("section", axis), route)


def gather_weights(shard, small):
    rows, width = shard.shape
    half = width // 2
    extra = jnp.concatenate([small[:, :half], small[:, half:]])
    own = [jnp.concatenate([shard[:, :half], extra]), shard[:, half:]]
    axes = ("y", "z")
    pieces = [jnp.stack([p, swap(p, "xh", 1)]) for p in own]
    for step in range(2):
        pieces = [jnp.concatenate([p, meet(p, a, step)]) for p, a in zip(pieces, axes)]
    small = jnp.sum(pieces[0][:, rows:].astype(F32), axis=0).astype(BF16)
    pieces = [p[:, :rows] for p in pieces]
    small, pieces = lax.optimization_barrier((small, pieces))
    come = [meet(p, a, 0) for p, a in zip(pieces, axes[::-1])]
    for step in range(2):
        small = small + meet(small, "z", step)
    small, come = lax.optimization_barrier((small, come))
    pieces = [jnp.concatenate([p, c]) for p, c in zip(pieces, come)]
    pieces = [(p, meet(p, a, 1)) for p, a in zip(pieces, axes[::-1])]
    whole = jnp.concatenate([small[:8], small[8:]], axis=1)
    return [*pieces[0], *pieces[1]], whole


def scatter_weights(parts, sums):
    axes = ("z", "y")
    sent, kept = parts[0::2], parts[1::2]
    moved = [meet(p, a, 0) for p, a in zip(sent, axes)]
    moved, sums = lax.optimization_barrier((moved, sums))
    half = sums.shape[1] // 2
    sums = jnp.concatenate([sums[:, :half], sums[:, half:]])
    grown = [k.astype(F32) + m.astype(F32) for k, m in zip(kept, moved)]
    onward = [g[:8].astype(BF16) for g in grown]
    onward, sums = lax.optimization_barrier((onward, sums))
    come = [meet(o, a, 1) for o, a in zip(onward, axes)]
    for step in range(2):
        sums = sums + meet(sums, "z", step)
    sums, come = lax.optimization_barrier((sums, come))
    blocks = [g[8:] + c.astype(F32) for g, c in zip(grown, come)]
    blocks[0] = jnp.concatenate([blocks[0], jnp.broadcast_to(sums, (8,) + sums.shape)], axis=1)
    own = []
    for b, axis in zip(blocks, axes[::-1]):
        b = b[4:] + meet(b[:4].astype(BF16), axis, 0).astype(F32)
        b = b[2:] + meet(b[:2].astype(BF16), axis, 1).astype(F32)
        own.append(b[0] + swap(b[1].astype(BF16), "xh", 1).astype(F32))
    rows = own[1].shape[0]
    sums = own[0][rows:]
    sums = jnp.concatenate([sums[:8], sums[8:]], axis=1)
    return jnp.concatenate([own[0][:rows], own[1]], axis=1), sums


def body(saved_inputs, grad_outputs, lengths, pointwise, depth_kernel, norm_gain):
    section = lax.axis_index("section")
    x, z, y = (lax.axis_index(a) for a in ("xh", "z", "y"))
    inputs = saved_inputs[0, :, 0]
    grads = grad_outputs[:, 0]
    lens = lengths[:, 0]
    micro, frames, features = inputs.shape
    factor = float(32 * micro * frames) ** (-0.5)

    at = section % 2 * 32 + x * 16 + z * 4 + y
    table = lax.dynamic_index_in_dim(jnp.asarray(tables()), at, 0, keepdims=False)
    meta = jnp.concatenate([section[None], lens, x[None], jnp.zeros((4,), jnp.int32), table])

    place = (x * 16 + z * 4 + y) * 48
    small = jnp.pad(jnp.concatenate([depth_kernel[0], norm_gain[0:1]], axis=0), ((0, 2), (0, 0)))
    small = lax.dynamic_update_slice(jnp.zeros((8, features), BF16), small, (0, place))
    weights, small = gather_weights(pointwise[0], small)
    taps = small.astype(F32)
    made = [forward(0, lens, inputs, taps)] * 2

    def turn(state, come, come_one, who):
        saved = [made[m][i] for i in range(3) for m in range(2)]
        return relay(who, meta, grads, come, come_one, weights, saved, taps, state)

    def hop(block, source):
        return lax.ppermute(block, "section", [(source, source - 1)])

    outs = [None] * 6
    outs[0], state = turn(None, made[0][0], made[0][0], (-1, -1, -1, 0))
    two_0 = hop(outs[0], 3)
    later, _ = lax.optimization_barrier((taps, outs[0]))
    made[1] = forward(1, lens, inputs, later)
    acts = [made[0][3], made[1][3]]
    outs[1], state = turn(state, two_0, two_0, (-1, -1, 0, 1))
    two_1, one_0 = hop(outs[1], 3), hop(outs[1], 2)
    outs[2], state = turn(state, two_1, two_1, (-1, -1, 1, -1))
    one_1 = hop(outs[2], 2)
    outs[3], state = turn(state, one_0, one_0, (-1, 0, -1, -1))
    outs[3], one_1 = lax.optimization_barrier((outs[3], one_1))
    zero_0 = hop(outs[3], 1)
    outs[4], state = turn(state, zero_0, one_1, (0, 1, -1, -1))
    zero_1 = hop(outs[4], 1)
    sums_0, _ = tap_terms(0, meta, inputs, *state, taps, outs[:0])
    zero_1, sums_0 = lax.optimization_barrier((zero_1, sums_0))
    parts = weight_terms(meta, acts, grads, [zero_0, zero_1, one_0, one_1, two_0, two_1])
    outs[5], state = turn(state, zero_1, zero_1, (1, -1, -1, -1))
    sums_1, frame_out = tap_terms(1, meta, inputs, *state, taps, outs)
    sums = sums_0 + sums_1

    point_share, sums = scatter_weights(parts, sums * factor)
    share = lax.dynamic_slice(sums, (0, place), (8, 48))
    return (
        frame_out[None, :, None],
        (point_share * factor)[None],
        share[None, :5],
        share[5:6],
    )


def solution(mesh):
    fine = Mesh(mesh.devices.reshape(4, 2, 4, 4), ("section", "xh", "z", "y"))
    fsdp = ("xh", "z", "y")
    return jax.shard_map(
        body,
        mesh=fine,
        in_specs=(
            P("section", None, fsdp, None, None),
            P(None, fsdp, None, None),
            P(None, fsdp),
            P("section", fsdp, None),
            P("section", None, fsdp),
            P("section", fsdp),
        ),
        out_specs=(
            P("section", None, fsdp, None, None),
            P("section", fsdp, None),
            P("section", None, fsdp),
            P("section", fsdp),
        ),
        check_vma=False,
    )
```

profile of v0, /device:TPU:0, one launch (start us, length us, event | category | flops | bytes accessed | tf_op | source)
XLA Modules:
  0.0 220.9 jit_solution(3917202916630348385)
XLA Ops:
  1.6 3.2 %collective-permute-start.3 = (bf16[48,768]{1,0:T(8,128)(2,1)S(1)}, bf16[48,768]{1,0:T(8,128)(2,1)S(1)}, u32[]{:S(2)}, u32[]{:S(2)}) collective-permute-start(bf16[48,768]{1,0:T(8,128)(2,1)S(1)} %get-tuple-element.115), channel_id=1, source_target_pairs={{0,16},{16,0},{1,17},{17,1},{2,18},{18,2},{3,19},{19,3},{4,20},{20... | collective-permute-start | bytes 221192 | tf_op jit(solution)/shard_map/ppermute | solution.py:517
  9.6 2.3 %collective-permute-done = bf16[64,768]{1,0:T(8,128)(2,1)S(1)} collective-permute-done((bf16[64,768]{1,0:T(8,128)(2,1)S(1)}, bf16[64,768]{1,0:T(8,128)(2,1)S(1)}, u32[]{:S(2)}, u32[]{:S(2)}) %collective-permute-start) | collective-permute-done | bytes 98336 | tf_op jit(solution)/shard_map/ppermute | solution.py:517
  13.7 4.1 %collective-permute-start.5 = (bf16[4,48,768]{2,1,0:T(8,128)(2,1)S(1)}, bf16[4,48,768]{2,1,0:T(8,128)(2,1)S(1)}, u32[]{:S(2)}, u32[]{:S(2)}) collective-permute-start(bf16[4,48,768]{2,1,0:T(8,128)(2,1)S(1)} %pad_maximum_fusion.6), channel_id=1, source_target_pairs={{0,12},{4,8},{8,4},{12,0},{32,36},{36,32},{40,44},{44,40},{64,76},... | collective-permute-start | bytes 884744 | tf_op jit(solution)/shard_map/ppermute | solution.py:527
  17.8 3.0 %collective-permute-start.2 = (bf16[4,64,768]{2,1,0:T(8,128)(2,1)S(1)}, bf16[4,64,768]{2,1,0:T(8,128)(2,1)S(1)}, u32[]{:S(2)}, u32[]{:S(2)}) collective-permute-start(bf16[4,64,768]{2,1,0:T(8,128)(2,1)S(1)} %pad_maximum_fusion.5), channel_id=1, source_target_pairs={{0,3},{1,2},{2,1},{3,0},{32,33},{33,32},{34,35},{35,34},{64,67},{6... | collective-permute-start | bytes 1179656 | tf_op jit(solution)/shard_map/ppermute | solution.py:527
  22.6 4.3 %collective-permute-done.2 = bf16[4,64,768]{2,1,0:T(8,128)(2,1)S(1)} collective-permute-done((bf16[4,64,768]{2,1,0:T(8,128)(2,1)S(1)}, bf16[4,64,768]{2,1,0:T(8,128)(2,1)S(1)}, u32[]{:S(2)}, u32[]{:S(2)}) %collective-permute-start.2) | collective-permute-done | bytes 393248 | tf_op jit(solution)/shard_map/ppermute | solution.py:527
  30.8 6.4 %collective-permute-done.6 = bf16[16,768]{1,0:T(8,128)(2,1)S(1)} collective-permute-done((bf16[16,768]{1,0:T(8,128)(2,1)S(1)}, bf16[16,768]{1,0:T(8,128)(2,1)S(1)}, u32[]{:S(2)}, u32[]{:S(2)}) %collective-permute-start.6) | collective-permute-done | bytes 24608 | tf_op jit(solution)/shard_map/ppermute | solution.py:527
  37.2 4.3 %collective-permute-start.7 = (bf16[16,768]{1,0:T(8,128)(2,1)S(1)}, bf16[16,768]{1,0:T(8,128)(2,1)S(1)}, u32[]{:S(2)}, u32[]{:S(2)}) collective-permute-start(bf16[16,768]{1,0:T(8,128)(2,1)S(1)} %add.82), channel_id=1, source_target_pairs={{0,12},{4,8},{8,4},{12,0},{32,36},{36,32},{40,44},{44,40},{64,76},... | collective-permute-start | bytes 73736 | tf_op jit(solution)/shard_map/ppermute | solution.py:527
  44.5 3.1 %collective-permute-start.11 = (bf16[16,48,768]{2,1,0:T(8,128)(2,1)S(1)}, bf16[16,48,768]{2,1,0:T(8,128)(2,1)S(1)}, u32[]{:S(2)}, u32[]{:S(2)}) collective-permute-start(bf16[16,48,768]{2,1,0:T(8,128)(2,1)S(1)} %constant_dynamic-update-slice_fusion.2.rest_2_), channel_id=1, source_target_pairs={{0,3},{1,2},{2,1},{3,0},{32,33},{33,32},{34,35},{35,34},{64,67},{6... | collective-permute-start | bytes 3538952 | tf_op jit(solution)/shard_map/ppermute | solution.py:527
  47.7 3.3 %collective-permute-start.10 = (bf16[16,48,768]{2,1,0:T(8,128)(2,1)S(1)}, bf16[16,48,768]{2,1,0:T(8,128)(2,1)}, u32[]{:S(2)}, u32[]{:S(2)}) collective-permute-start(bf16[16,48,768]{2,1,0:T(8,128)(2,1)S(1)} %constant_dynamic-update-slice_fusion.rest_0_), channel_id=1, source_target_pairs={{0,12},{4,8},{8,4},{12,0},{32,36},{36,32},{40,44},{44,40},{64,76},... | collective-permute-start | bytes 3538952 | tf_op jit(solution)/shard_map/ppermute | solution.py:527
  51.6 9.3 %shard_map.102 = (bf16[512,1536]{1,0:T(8,128)(2,1)}, bf16[512,1536]{1,0:T(8,128)(2,1)}, f32[512,128]{1,0:T(8,128)}, bf16[1536,512]{1,0:T(8,128)(2,1)}) custom-call(s32[2]{0:T(128)} %bitcast.54, bf16[2,512,1536]{2,1,0:T(8,128)(2,1)} %bitcast.57, f32[8,1536]{1,0:T(8,128)} %maximum_convert_fusion.taps.rest_10_), custom_call_target="tpu_custom_call" | custom-call | flops 8000000000 | bytes 1048576 | tf_op jit(solution)/shard_map/pallas_call | solution.py:131
  62.0 3.3 %collective-permute-done.10.rest_1_ = bf16[16,48,768]{2,1,0:T(8,128)(2,1)} collective-permute-done((bf16[16,48,768]{2,1,0:T(8,128)(2,1)S(1)}, bf16[16,48,768]{2,1,0:T(8,128)(2,1)}, u32[]{:S(2)}, u32[]{:S(2)}) %collective-permute-start.10) | collective-permute-done | bytes 1179680 | tf_op jit(solution)/shard_map/ppermute | solution.py:527
  67.0 9.4 %shard_map.104 = (bf16[512,1536]{1,0:T(8,128)(2,1)}, bf16[512,1536]{1,0:T(8,128)(2,1)}, f32[512,128]{1,0:T(8,128)}, bf16[1536,512]{1,0:T(8,128)(2,1)}) custom-call(s32[2]{0:T(128)} %bitcast.55, bf16[2,512,1536]{2,1,0:T(8,128)(2,1)} %bitcast.58, f32[8,1536]{1,0:T(8,128)} %maximum_convert_fusion.taps.rest_10_), custom_call_target="tpu_custom_call" | custom-call | flops 8000000000 | bytes 1048576 | tf_op jit(solution)/shard_map/pallas_call | solution.py:131
  86.6 44.6 %collective-permute-done.16.come.rest_1_ = bf16[512,1536]{1,0:T(8,128)(2,1)S(1)} collective-permute-done((bf16[512,1536]{1,0:T(8,128)(2,1)}, bf16[512,1536]{1,0:T(8,128)(2,1)S(1)}, u32[]{:S(2)}, u32[]{:S(2)}) %collective-permute-start.16) | collective-permute-done | bytes 1572896 | tf_op jit(solution)/shard_map/ppermute | solution.py:604
  132.4 10.3 %shard_map.108 = (bf16[512,1536]{1,0:T(8,128)(2,1)}, bf16[2,512,1536]{2,1,0:T(8,128)(2,1)}, f32[2,8,1536]{2,1,0:T(8,128)}) custom-call(s32[136]{0:T(256)} %concatenate.57.meta, bf16[2,512,1536]{2,1,0:T(8,128)(2,1)} %bitcast.42, bf16[512,1536]{1,0:T(8,128)(2,1)} %copy-done.8, ...), custom_call_target="tpu_custom_call", output_to_operand_aliasing={{1}: (15, {}), {2}: (16, {})} | custom-call | flops 1000000000 | bytes 1048576 | tf_op jit(solution)/shard_map/pallas_call | solution.py:323
  144.0 5.1 %shard_map.109 = f32[8,1536]{1,0:T(8,128)} custom-call(s32[136]{0:T(256)} %concatenate.57.meta, bf16[2,512,1536]{2,1,0:T(8,128)(2,1)} %bitcast.59, bf16[2,512,1536]{2,1,0:T(8,128)(2,1)} %get-tuple-element.84.mixed_in.rest_11_, f32[2,8,1536]{2,1,0:T(8,128)} %get-tuple-element.85.gain_in.rest_12_, f32[8,1536]{1,0:T(8,128)} %maximum_convert_fusion.taps.rest_10_), custom_call_target="tpu_custom_call" | custom-call | flops 5000000000 | bytes 1048576 | tf_op jit(solution)/shard_map/pallas_call | solution.py:495
  150.2 11.3 %shard_map.112 = (bf16[16,48,768]{2,1,0:T(8,128)(2,1)}, bf16[16,48,768]{2,1,0:T(8,128)(2,1)}, bf16[16,48,768]{2,1,0:T(8,128)(2,1)}, bf16[16,48,768]{2,1,0:T(8,128)(2,1)}) custom-call(s32[136]{0:T(256)} %concatenate.57.meta, bf16[1536,512]{1,0:T(8,128)(2,1)} %get-tuple-element.91.act_a, bf16[1536,512]{1,0:T(8,128)(2,1)} %get-tuple-element.92.act_b, ...), custom_call_target="tpu_custom_call" | custom-call | flops 8000000000 | bytes 1048576 | tf_op jit(solution)/shard_map/pallas_call | solution.py:405
  161.8 10.5 %shard_map.110 = (bf16[512,1536]{1,0:T(8,128)(2,1)}, bf16[2,512,1536]{2,1,0:T(8,128)(2,1)}, f32[2,8,1536]{2,1,0:T(8,128)}) custom-call(s32[136]{0:T(256)} %concatenate.57.meta, bf16[2,512,1536]{2,1,0:T(8,128)(2,1)} %bitcast.44, bf16[512,1536]{1,0:T(8,128)(2,1)} %copy-done.6, ...), custom_call_target="tpu_custom_call", output_to_operand_aliasing={{1}: (15, {}), {2}: (16, {})} | custom-call | flops 1000000000 | bytes 1048576 | tf_op jit(solution)/shard_map/pallas_call | solution.py:323
  172.3 6.2 %shard_map.111 = (f32[8,1536]{1,0:T(8,128)}, bf16[2,512,1536]{2,1,0:T(8,128)(2,1)}) custom-call(s32[136]{0:T(256)} %concatenate.57.meta, bf16[2,512,1536]{2,1,0:T(8,128)(2,1)} %bitcast.60, bf16[2,512,1536]{2,1,0:T(8,128)(2,1)} %get-tuple-element.87.mixed_in, f32[2,8,1536]{2,1,0:T(8,128)} %get-tuple-element.88.gain_in, ...), custom_call_target="tpu_custom_call" | custom-call | flops 5000000000 | bytes 1048576 | tf_op jit(solution)/shard_map/pallas_call | solution.py:495
  181.6 3.3 %collective-permute-start.22 = (bf16[8,48,768]{2,1,0:T(8,128)(2,1)S(1)}, bf16[8,48,768]{2,1,0:T(8,128)(2,1)S(1)}, u32[]{:S(2)}, u32[]{:S(2)}) collective-permute-start(bf16[8,48,768]{2,1,0:T(8,128)(2,1)S(1)} %slice.194), channel_id=1, source_target_pairs={{0,12},{4,8},{8,4},{12,0},{32,36},{36,32},{40,44},{44,40},{64,76},... | collective-permute-start | bytes 1769480 | tf_op jit(solution)/shard_map/ppermute | solution.py:527
  187.8 3.6 %collective-permute-done.20 = f32[16,768]{1,0:T(8,128)S(1)} collective-permute-done((f32[16,768]{1,0:T(8,128)S(1)}, f32[16,768]{1,0:T(8,128)S(1)}, u32[]{:S(2)}, u32[]{:S(2)}) %collective-permute-start.20) | collective-permute-done | bytes 49184 | tf_op jit(solution)/shard_map/ppermute | solution.py:527
  191.7 5.0 %collective-permute-done.21 = f32[16,768]{1,0:T(8,128)S(1)} collective-permute-done((f32[16,768]{1,0:T(8,128)S(1)}, f32[16,768]{1,0:T(8,128)S(1)}, u32[]{:S(2)}, u32[]{:S(2)}) %collective-permute-start.21) | collective-permute-done | bytes 49184 | tf_op jit(solution)/shard_map/ppermute | solution.py:527
  198.6 5.1 %collective-permute-done.27 = bf16[4,48,768]{2,1,0:T(8,128)(2,1)S(1)} collective-permute-done((bf16[4,48,768]{2,1,0:T(8,128)(2,1)S(1)}, bf16[4,48,768]{2,1,0:T(8,128)(2,1)S(1)}, u32[]{:S(2)}, u32[]{:S(2)}) %collective-permute-start.27) | collective-permute-done | bytes 294944 | tf_op jit(solution)/shard_map/ppermute | solution.py:527
  207.7 2.5 %collective-permute-done.28 = bf16[2,48,768]{2,1,0:T(8,128)(2,1)S(1)} collective-permute-done((bf16[2,48,768]{2,1,0:T(8,128)(2,1)S(1)}, bf16[2,48,768]{2,1,0:T(8,128)(2,1)S(1)}, u32[]{:S(2)}, u32[]{:S(2)}) %collective-permute-start.28) | collective-permute-done | bytes 147488 | tf_op jit(solution)/shard_map/ppermute | solution.py:527
  216.2 2.7 %collective-permute-done.26 = bf16[64,768]{1,0:T(8,128)(2,1)S(1)} collective-permute-done((bf16[64,768]{1,0:T(8,128)(2,1)S(1)}, bf16[64,768]{1,0:T(8,128)(2,1)S(1)}, u32[]{:S(2)}, u32[]{:S(2)}) %collective-permute-start.26) | collective-permute-done | bytes 98336 | tf_op jit(solution)/shard_map/ppermute | solution.py:517
  (127 shorter events, 53.2 us)
Async XLA Ops:
  1.6 5.9 %collective-permute-start.3 = (bf16[48,768]{1,0:T(8,128)(2,1)S(1)}, bf16[48,768]{1,0:T(8,128)(2,1)S(1)}, u32[]{:S(2)}, u32[]{:S(2)}) collective-permute-start(bf16[48,768]{1,0:T(8,128)(2,1)S(1)} %get-tuple-element.115), channel_id=1, source_target_pairs={{0,16},{16,0},{1,17},{17,1},{2,18},{18,2},{3,19},{19,3},{4,20},{20... | collective-permute-start | bytes 221192 | tf_op jit(solution)/shard_map/ppermute | solution.py:517
  5.7 6.2 %collective-permute-start = (bf16[64,768]{1,0:T(8,128)(2,1)S(1)}, bf16[64,768]{1,0:T(8,128)(2,1)S(1)}, u32[]{:S(2)}, u32[]{:S(2)}) collective-permute-start(bf16[64,768]{1,0:T(8,128)(2,1)S(1)} %get-tuple-element.118), channel_id=1, source_target_pairs={{0,16},{16,0},{1,17},{17,1},{2,18},{18,2},{3,19},{19,3},{4,20},{20... | collective-permute-start | bytes 294920 | tf_op jit(solution)/shard_map/ppermute | solution.py:517
  7.5 6.1 %collective-permute-start.4 = (bf16[2,48,768]{2,1,0:T(8,128)(2,1)S(1)}, bf16[2,48,768]{2,1,0:T(8,128)(2,1)S(1)}, u32[]{:S(2)}, u32[]{:S(2)}) collective-permute-start(bf16[2,48,768]{2,1,0:T(8,128)(2,1)S(1)} %pad_maximum_fusion.8), channel_id=1, source_target_pairs={{0,4},{4,0},{8,12},{12,8},{32,44},{36,40},{40,36},{44,32},{64,68},... | collective-permute-start | bytes 442376 | tf_op jit(solution)/shard_map/ppermute | solution.py:527
  13.7 8.8 %collective-permute-start.5 = (bf16[4,48,768]{2,1,0:T(8,128)(2,1)S(1)}, bf16[4,48,768]{2,1,0:T(8,128)(2,1)S(1)}, u32[]{:S(2)}, u32[]{:S(2)}) collective-permute-start(bf16[4,48,768]{2,1,0:T(8,128)(2,1)S(1)} %pad_maximum_fusion.6), channel_id=1, source_target_pairs={{0,12},{4,8},{8,4},{12,0},{32,36},{36,32},{40,44},{44,40},{64,76},... | collective-permute-start | bytes 884744 | tf_op jit(solution)/shard_map/ppermute | solution.py:527
  17.8 9.1 %collective-permute-start.2 = (bf16[4,64,768]{2,1,0:T(8,128)(2,1)S(1)}, bf16[4,64,768]{2,1,0:T(8,128)(2,1)S(1)}, u32[]{:S(2)}, u32[]{:S(2)}) collective-permute-start(bf16[4,64,768]{2,1,0:T(8,128)(2,1)S(1)} %pad_maximum_fusion.5), channel_id=1, source_target_pairs={{0,3},{1,2},{2,1},{3,0},{32,33},{33,32},{34,35},{35,34},{64,67},{6... | collective-permute-start | bytes 1179656 | tf_op jit(solution)/shard_map/ppermute | solution.py:527
  27.0 16.4 %collective-permute-start.8 = (bf16[8,48,768]{2,1,0:T(8,128)(2,1)S(1)}, bf16[8,48,768]{2,1,0:T(8,128)(2,1)S(1)}, u32[]{:S(2)}, u32[]{:S(2)}) collective-permute-start(bf16[8,48,768]{2,1,0:T(8,128)(2,1)S(1)} %pad_maximum_fusion.1), channel_id=1, source_target_pairs={{0,4},{4,0},{8,12},{12,8},{32,44},{36,40},{40,36},{44,32},{64,68},... | collective-permute-start | bytes 1769480 | tf_op jit(solution)/shard_map/ppermute | solution.py:527
  28.9 14.5 %collective-permute-start.9 = (bf16[8,48,768]{2,1,0:T(8,128)(2,1)S(1)}, bf16[8,48,768]{2,1,0:T(8,128)(2,1)}, u32[]{:S(2)}, u32[]{:S(2)}) collective-permute-start(bf16[8,48,768]{2,1,0:T(8,128)(2,1)S(1)} %pad_maximum_fusion.4), channel_id=1, source_target_pairs={{0,1},{1,0},{2,3},{3,2},{32,35},{33,34},{34,33},{35,32},{64,65},{6... | collective-permute-start | bytes 1769480 | tf_op jit(solution)/shard_map/ppermute | solution.py:527
  30.6 6.6 %collective-permute-start.6 = (bf16[16,768]{1,0:T(8,128)(2,1)S(1)}, bf16[16,768]{1,0:T(8,128)(2,1)S(1)}, u32[]{:S(2)}, u32[]{:S(2)}) collective-permute-start(bf16[16,768]{1,0:T(8,128)(2,1)S(1)} %maximum_reduce_fusion), channel_id=1, source_target_pairs={{0,4},{4,0},{8,12},{12,8},{32,44},{36,40},{40,36},{44,32},{64,68},... | collective-permute-start | bytes 73736 | tf_op jit(solution)/shard_map/ppermute | solution.py:527
  37.2 6.1 %collective-permute-start.7 = (bf16[16,768]{1,0:T(8,128)(2,1)S(1)}, bf16[16,768]{1,0:T(8,128)(2,1)S(1)}, u32[]{:S(2)}, u32[]{:S(2)}) collective-permute-start(bf16[16,768]{1,0:T(8,128)(2,1)S(1)} %add.82), channel_id=1, source_target_pairs={{0,12},{4,8},{8,4},{12,0},{32,36},{36,32},{40,44},{44,40},{64,76},... | collective-permute-start | bytes 73736 | tf_op jit(solution)/shard_map/ppermute | solution.py:527
  44.5 17.5 %collective-permute-start.11 = (bf16[16,48,768]{2,1,0:T(8,128)(2,1)S(1)}, bf16[16,48,768]{2,1,0:T(8,128)(2,1)S(1)}, u32[]{:S(2)}, u32[]{:S(2)}) collective-permute-start(bf16[16,48,768]{2,1,0:T(8,128)(2,1)S(1)} %constant_dynamic-update-slice_fusion.2.rest_2_), channel_id=1, source_target_pairs={{0,3},{1,2},{2,1},{3,0},{32,33},{33,32},{34,35},{35,34},{64,67},{6... | collective-permute-start | bytes 3538952 | tf_op jit(solution)/shard_map/ppermute | solution.py:527
  47.7 17.6 %collective-permute-start.10 = (bf16[16,48,768]{2,1,0:T(8,128)(2,1)S(1)}, bf16[16,48,768]{2,1,0:T(8,128)(2,1)}, u32[]{:S(2)}, u32[]{:S(2)}) collective-permute-start(bf16[16,48,768]{2,1,0:T(8,128)(2,1)S(1)} %constant_dynamic-update-slice_fusion.rest_0_), channel_id=1, source_target_pairs={{0,12},{4,8},{8,4},{12,0},{32,36},{36,32},{40,44},{44,40},{64,76},... | collective-permute-start | bytes 3538952 | tf_op jit(solution)/shard_map/ppermute | solution.py:527
  66.2 10.2 %collective-permute-start.12 = (bf16[512,1536]{1,0:T(8,128)(2,1)}, bf16[512,1536]{1,0:T(8,128)(2,1)S(1)}, u32[]{:S(2)}, u32[]{:S(2)}) collective-permute-start(bf16[512,1536]{1,0:T(8,128)(2,1)} %get-tuple-element.65.rest_0_), channel_id=1, source_target_pairs={{96,64},{97,65},{98,66},{99,67},{100,68},{101,69},{102,70},{103,71... | collective-permute-start | bytes 4718600 | tf_op jit(solution)/shard_map/ppermute | solution.py:604
  85.3 45.9 %collective-permute-start.16 = (bf16[512,1536]{1,0:T(8,128)(2,1)}, bf16[512,1536]{1,0:T(8,128)(2,1)S(1)}, u32[]{:S(2)}, u32[]{:S(2)}) collective-permute-start(bf16[512,1536]{1,0:T(8,128)(2,1)} %get-tuple-element.79.rest_3_), channel_id=1, source_target_pairs={{32,0},{33,1},{34,2},{35,3},{36,4},{37,5},{38,6},{39,7},{40,8},{41... | collective-permute-start | bytes 4718600 | tf_op jit(solution)/shard_map/ppermute | solution.py:604
  142.7 6.4 %collective-permute-start.17 = (bf16[512,1536]{1,0:T(8,128)(2,1)}, bf16[512,1536]{1,0:T(8,128)(2,1)S(1)}, u32[]{:S(2)}, u32[]{:S(2)}) collective-permute-start(bf16[512,1536]{1,0:T(8,128)(2,1)} %get-tuple-element.83.rest_4_), channel_id=1, source_target_pairs={{32,0},{33,1},{34,2},{35,3},{36,4},{37,5},{38,6},{39,7},{40,8},{41... | collective-permute-start | bytes 4718600 | tf_op jit(solution)/shard_map/ppermute | solution.py:604
  161.6 17.8 %collective-permute-start.18 = (bf16[16,48,768]{2,1,0:T(8,128)(2,1)}, bf16[16,48,768]{2,1,0:T(8,128)(2,1)S(1)}, u32[]{:S(2)}, u32[]{:S(2)}) collective-permute-start(bf16[16,48,768]{2,1,0:T(8,128)(2,1)} %get-tuple-element.94), channel_id=1, source_target_pairs={{0,4},{4,0},{8,12},{12,8},{32,44},{36,40},{40,36},{44,32},{64,68},... | collective-permute-start | bytes 3538952 | tf_op jit(solution)/shard_map/ppermute | solution.py:527
  161.7 17.7 %collective-permute-start.19 = (bf16[16,48,768]{2,1,0:T(8,128)(2,1)}, bf16[16,48,768]{2,1,0:T(8,128)(2,1)}, u32[]{:S(2)}, u32[]{:S(2)}) collective-permute-start(bf16[16,48,768]{2,1,0:T(8,128)(2,1)} %get-tuple-element.95), channel_id=1, source_target_pairs={{0,1},{1,0},{2,3},{3,2},{32,35},{33,34},{34,33},{35,32},{64,65},{6... | collective-permute-start | bytes 3538952 | tf_op jit(solution)/shard_map/ppermute | solution.py:527
  181.6 15.2 %collective-permute-start.22 = (bf16[8,48,768]{2,1,0:T(8,128)(2,1)S(1)}, bf16[8,48,768]{2,1,0:T(8,128)(2,1)S(1)}, u32[]{:S(2)}, u32[]{:S(2)}) collective-permute-start(bf16[8,48,768]{2,1,0:T(8,128)(2,1)S(1)} %slice.194), channel_id=1, source_target_pairs={{0,12},{4,8},{8,4},{12,0},{32,36},{36,32},{40,44},{44,40},{64,76},... | collective-permute-start | bytes 1769480 | tf_op jit(solution)/shard_map/ppermute | solution.py:527
  184.9 11.9 %collective-permute-start.23 = (bf16[8,48,768]{2,1,0:T(8,128)(2,1)S(1)}, bf16[8,48,768]{2,1,0:T(8,128)(2,1)S(1)}, u32[]{:S(2)}, u32[]{:S(2)}) collective-permute-start(bf16[8,48,768]{2,1,0:T(8,128)(2,1)S(1)} %slice.193), channel_id=1, source_target_pairs={{0,3},{1,2},{2,1},{3,0},{32,33},{33,32},{34,35},{35,34},{64,67},{6... | collective-permute-start | bytes 1769480 | tf_op jit(solution)/shard_map/ppermute | solution.py:527
  196.9 6.8 %collective-permute-start.27 = (bf16[4,48,768]{2,1,0:T(8,128)(2,1)S(1)}, bf16[4,48,768]{2,1,0:T(8,128)(2,1)S(1)}, u32[]{:S(2)}, u32[]{:S(2)}) collective-permute-start(bf16[4,48,768]{2,1,0:T(8,128)(2,1)S(1)} %slice.195), channel_id=1, source_target_pairs={{0,4},{4,0},{8,12},{12,8},{32,44},{36,40},{40,36},{44,32},{64,68},... | collective-permute-start | bytes 884744 | tf_op jit(solution)/shard_map/ppermute | solution.py:527
  197.7 7.9 %collective-permute-start.24 = (bf16[4,64,768]{2,1,0:T(8,128)(2,1)S(1)}, bf16[4,64,768]{2,1,0:T(8,128)(2,1)S(1)}, u32[]{:S(2)}, u32[]{:S(2)}) collective-permute-start(bf16[4,64,768]{2,1,0:T(8,128)(2,1)S(1)} %fusion.2), channel_id=1, source_target_pairs={{0,1},{1,0},{2,3},{3,2},{32,35},{33,34},{34,33},{35,32},{64,65},{6... | collective-permute-start | bytes 1179656 | tf_op jit(solution)/shard_map/ppermute | solution.py:527
  203.8 6.4 %collective-permute-start.28 = (bf16[2,48,768]{2,1,0:T(8,128)(2,1)S(1)}, bf16[2,48,768]{2,1,0:T(8,128)(2,1)S(1)}, u32[]{:S(2)}, u32[]{:S(2)}) collective-permute-start(bf16[2,48,768]{2,1,0:T(8,128)(2,1)S(1)} %slice.197), channel_id=1, source_target_pairs={{0,12},{4,8},{8,4},{12,0},{32,36},{36,32},{40,44},{44,40},{64,76},... | collective-permute-start | bytes 442376 | tf_op jit(solution)/shard_map/ppermute | solution.py:527
  205.7 7.0 %collective-permute-start.25 = (bf16[2,64,768]{2,1,0:T(8,128)(2,1)S(1)}, bf16[2,64,768]{2,1,0:T(8,128)(2,1)S(1)}, u32[]{:S(2)}, u32[]{:S(2)}) collective-permute-start(bf16[2,64,768]{2,1,0:T(8,128)(2,1)S(1)} %slice.196), channel_id=1, source_target_pairs={{0,3},{1,2},{2,1},{3,0},{32,33},{33,32},{34,35},{35,34},{64,67},{6... | collective-permute-start | bytes 589832 | tf_op jit(solution)/shard_map/ppermute | solution.py:527
  210.3 5.9 %collective-permute-start.29 = (bf16[48,768]{1,0:T(8,128)(2,1)S(1)}, bf16[48,768]{1,0:T(8,128)(2,1)S(1)}, u32[]{:S(2)}, u32[]{:S(2)}) collective-permute-start(bf16[48,768]{1,0:T(8,128)(2,1)S(1)} %fusion.7), channel_id=1, source_target_pairs={{0,16},{16,0},{1,17},{17,1},{2,18},{18,2},{3,19},{19,3},{4,20},{20... | collective-permute-start | bytes 221192 | tf_op jit(solution)/shard_map/ppermute | solution.py:517
  212.7 6.2 %collective-permute-start.26 = (bf16[64,768]{1,0:T(8,128)(2,1)S(1)}, bf16[64,768]{1,0:T(8,128)(2,1)S(1)}, u32[]{:S(2)}, u32[]{:S(2)}) collective-permute-start(bf16[64,768]{1,0:T(8,128)(2,1)S(1)} %fusion.6), channel_id=1, source_target_pairs={{0,16},{16,0},{1,17},{17,1},{2,18},{18,2},{3,19},{19,3},{4,20},{20... | collective-permute-start | bytes 294920 | tf_op jit(solution)/shard_map/ppermute | solution.py:517
  (19 other events, 137.1 us)
where the time goes:
time: 222 us; the launch traced here: 221 us
  waiting for transfers between devices  88.7 us (40%)
  Pallas kernels  66.1 us (30%)
  starting transfers between devices  48.2 us (22%)
  local copies, waits for them, and re-layouts  10.9 us (5%)
  other arithmetic  5.7 us (3%)
    ppermute x6, waiting for transfers between devices, hop(): return lax.ppermute(block, 'section', [(source, source - 1)])  44.7 us
    ppermute x20, waiting for transfers between devices, meet(): return lax.ppermute(x, ('section', axis), route)  36.4 us
    ppermute x20, starting transfers between devices, meet(): return lax.ppermute(x, ('section', axis), route)  34.7 us
    pallas_call x6, Pallas kernels, relay(): pl.pallas_call(functools.partial(relay_kernel, first, who), in_specs=spec...  24.7 us
    pallas_call x2, Pallas kernels, forward(): pl.pallas_call(functools.partial(forward_kernel, m), in_specs=[SMEM, HBM,...  18.8 us
    pallas_call x2, Pallas kernels, tap_terms(): pl.pallas_call(functools.partial(tap_kernel, m), in_specs=[SMEM, HBM, HBM...  11.4 us
    pallas_call x1, Pallas kernels, weight_terms(): pl.pallas_call(weight_kernel, in_specs=[SMEM, ANY, ANY, HBM] + [ANY] * le...  11.3 us
    ppermute x4, starting transfers between devices, swap(): return lax.ppermute(x, axis, [(i, i ^ d) for i in range(n)])  7.83 us
  transfers between devices with their start and end apart: 30, of which 17 were waited for; matrix products, arithmetic and copies ran while one was open for 2% of the time, Pallas kernels for 19%

commit v1 on v0

--- a/solution.py
+++ b/solution.py
@@ -57,7 +57,7 @@
 
 
 def forward_kernel(m, lens, x_in, taps, normed_out, slope_out, inv_out, act_out, *rest):
-    x_ref, hid, mix, normed_ref, slope_ref, inv_ref, act, act_ref, sem, sems = rest
+    x_ref, hid, mix, normed_ref, slope_ref, inv_ref, act, act_ref, low, sem, sems = rest
     length = lens[m]
     frames, feats = x_ref.shape
     cols = feats // LANES
@@ -81,31 +81,49 @@
 
     def conv(i, carry):
         r = pl.multiple_of(i * 64, 64)
+        whole = jnp.zeros((64, LANES), F32)
         for c in range(cols):
             span = slice(c * LANES, (c + 1) * LANES)
             total = taps[0:1, span] * hid[c, pl.ds(r + PAD - 2, 64), :]
             for k in range(1, 5):
                 total = total + taps[k : k + 1, span] * hid[c, pl.ds(r + PAD - 2 + k, 64), :]
             mix[pl.ds(r, 64), span] = total
+            whole = whole + total
+        mean = jnp.sum(whole, axis=-1, keepdims=True) * (1.0 / feats)
+        low[pl.ds(r, 64), :] = jnp.broadcast_to(mean, (64, LANES))
         return carry
 
     lax.fori_loop(0, frames // 64, conv, 0)
+
+    def centre(i, carry):
+        r = pl.multiple_of(i * 64, 64)
+        mean = low[pl.ds(r, 64), :]
+        whole = jnp.zeros((64, LANES), F32)
+        for c in range(cols):
+            span = slice(c * LANES, (c + 1) * LANES)
+            centred = mix[pl.ds(r, 64), span] - mean
+            mix[pl.ds(r, 64), span] = centred
+            whole = whole + centred * centred
+        spread = jnp.sum(whole, axis=-1, keepdims=True) * (1.0 / feats)
+        inv_ref[pl.ds(r, 64), :] = jnp.broadcast_to(lax.rsqrt(spread + EPSILON), (64, LANES))
+        return carry
+
+    lax.fori_loop(0, frames // 64, centre, 0, unroll=2)
 
     def norm(i, carry):
         r = pl.multiple_of(i * 16, 16)
-        keep = r + lax.broadcasted_iota(jnp.int32, (16, 1), 0) < length
-        mixed = mix[pl.ds(r, 16), :]
-        centred = mixed - jnp.mean(mixed, axis=-1, keepdims=True)
-        inverse = lax.rsqrt(jnp.mean(centred * centred, axis=-1, keepdims=True) + EPSILON)
-        gain = taps[5:6, :]
-        normed = centred * inverse
-        gained = normed * gain
-        logistic = jax.nn.sigmoid(gained)
-        normed_ref[pl.ds(r, 16), :] = normed.astype(BF16)
-        slope = (logistic + gained * logistic * (1.0 - logistic)) * gain
-        slope_ref[pl.ds(r, 16), :] = jnp.where(keep, slope, 0.0).astype(BF16)
-        act[pl.ds(r, 16), :] = jnp.where(keep, gained * logistic, 0.0).astype(BF16)
-        inv_ref[pl.ds(r, 16), :] = jnp.broadcast_to(inverse, (16, LANES))
+        keep = r + lax.broadcasted_iota(jnp.int32, (16, LANES), 0) < length
+        inverse = inv_ref[pl.ds(r, 16), :]
+        for c in range(cols):
+            span = slice(c * LANES, (c + 1) * LANES)
+            gain = taps[5:6, span]
+            normed = mix[pl.ds(r, 16), span] * inverse
+            gained = normed * gain
+            logistic = jax.nn.sigmoid(gained)
+            normed_ref[pl.ds(r, 16), span] = normed.astype(BF16)
+            slope = (logistic + gained * logistic * (1.0 - logistic)) * gain
+            slope_ref[pl.ds(r, 16), span] = jnp.where(keep, slope, 0.0).astype(BF16)
+            act[pl.ds(r, 16), span] = jnp.where(keep, gained * logistic, 0.0).astype(BF16)
         return carry
 
     outs = ((normed_ref, normed_out), (slope_ref, slope_out), (inv_ref, inv_out))
@@ -147,6 +165,7 @@
             pltpu.VMEM((frames, LANES), F32),
             pltpu.VMEM((frames, feats), BF16),
             pltpu.VMEM((feats, frames), BF16),
+            pltpu.VMEM((frames, LANES), F32),
             pltpu.SemaphoreType.DMA,
             pltpu.SemaphoreType.DMA((4,)),
         ],
@@ -512,6 +531,18 @@
     return made[0], (made[1] if more else None)
 
 
+def early(x):
+    return pl.pallas_call(
+        lambda x_ref, out_ref: None,
+        in_specs=[ANY],
+        out_specs=ANY,
+        out_shape=jax.ShapeDtypeStruct(x.shape, x.dtype),
+        input_output_aliases={0: 0},
+        compiler_params=params(60),
+        cost_estimate=cost(30),
+    )(x)
+
+
 def swap(x, axis, d):
     n = lax.axis_size(axis)
     return lax.ppermute(x, axis, [(i, i ^ d) for i in range(n)])
@@ -527,7 +558,7 @@
     return lax.ppermute(x, ("section", axis), route)
 
 
-def gather_weights(shard, small):
+def gather_weights(shard, small, run):
     rows, width = shard.shape
     half = width // 2
     extra = jnp.concatenate([small[:, :half], small[:, half:]])
@@ -537,16 +568,18 @@
     for step in range(2):
         pieces = [jnp.concatenate([p, meet(p, a, step)]) for p, a in zip(pieces, axes)]
     small = jnp.sum(pieces[0][:, rows:].astype(F32), axis=0).astype(BF16)
+    for step in range(2):
+        small = small + meet(small, "z", step)
     pieces = [p[:, :rows] for p in pieces]
     small, pieces = lax.optimization_barrier((small, pieces))
     come = [meet(p, a, 0) for p, a in zip(pieces, axes[::-1])]
-    for step in range(2):
-        small = small + meet(small, "z", step)
-    small, come = lax.optimization_barrier((small, come))
+    whole = jnp.concatenate([small[:8], small[8:]], axis=1).astype(F32)
+    made = [run(0, whole)]
+    made, come, whole = lax.optimization_barrier((made, come, whole))
     pieces = [jnp.concatenate([p, c]) for p, c in zip(pieces, come)]
     pieces = [(p, meet(p, a, 1)) for p, a in zip(pieces, axes[::-1])]
-    whole = jnp.concatenate([small[:8], small[8:]], axis=1)
-    return [*pieces[0], *pieces[1]], whole
+    made.append(run(1, whole))
+    return [*pieces[0], *pieces[1]], whole, made
 
 
 def scatter_weights(parts, sums):
@@ -592,9 +625,10 @@
     place = (x * 16 + z * 4 + y) * 48
     small = jnp.pad(jnp.concatenate([depth_kernel[0], norm_gain[0:1]], axis=0), ((0, 2), (0, 0)))
     small = lax.dynamic_update_slice(jnp.zeros((8, features), BF16), small, (0, place))
-    weights, small = gather_weights(pointwise[0], small)
-    taps = small.astype(F32)
-    made = [forward(0, lens, inputs, taps)] * 2
+
+    weights, taps, made = gather_weights(
+        pointwise[0], small, lambda m, taps: forward(m, lens, inputs, taps)
+    )
 
     def turn(state, come, come_one, who):
         saved = [made[m][i] for i in range(3) for m in range(2)]
@@ -606,16 +640,14 @@
     outs = [None] * 6
     outs[0], state = turn(None, made[0][0], made[0][0], (-1, -1, -1, 0))
     two_0 = hop(outs[0], 3)
-    later, _ = lax.optimization_barrier((taps, outs[0]))
-    made[1] = forward(1, lens, inputs, later)
     acts = [made[0][3], made[1][3]]
     outs[1], state = turn(state, two_0, two_0, (-1, -1, 0, 1))
     two_1, one_0 = hop(outs[1], 3), hop(outs[1], 2)
     outs[2], state = turn(state, two_1, two_1, (-1, -1, 1, -1))
     one_1 = hop(outs[2], 2)
     outs[3], state = turn(state, one_0, one_0, (-1, 0, -1, -1))
-    outs[3], one_1 = lax.optimization_barrier((outs[3], one_1))
     zero_0 = hop(outs[3], 1)
+    one_1 = early(one_1)
     outs[4], state = turn(state, zero_0, one_1, (0, 1, -1, -1))
     zero_1 = hop(outs[4], 1)
     sums_0, _ = tap_terms(0, meta, inputs, *state, taps, outs[:0])

time: 222 us -> 220 us (level)
  waiting for transfers between devices: 88.7 us -> 82.6 us
  starting transfers between devices: 48.2 us -> 52.1 us
    ppermute x20, waiting for transfers between devices: 36.4 us -> 29.6 us  [meet(): return lax.ppermute(x, ('section', axis), route)]
    ppermute x20, starting transfers between devices: 34.7 us -> 37.1 us  [meet(): return lax.ppermute(x, ('section', axis), route)]
  transfers between devices with their start and end apart: 30 -> 30, of which waited for: 17 -> 20; matrix products, arithmetic and copies ran while one was open for 2% -> 2% of each run, Pallas kernels for 19% -> 19%
where the time goes in v1:
time: 220 us; the launch traced here: 219 us
  waiting for transfers between devices  82.6 us (38%)
  Pallas kernels  64.1 us (29%)
  starting transfers between devices  52.1 us (24%)
  local copies, waits for them, and re-layouts  13.1 us (6%)
  other arithmetic  5.7 us (3%)
    ppermute x6, waiting for transfers between devices, hop(): return lax.ppermute(block, 'section', [(source, source - 1)])  45.1 us
    ppermute x20, starting transfers between devices, meet(): return lax.ppermute(x, ('section', axis), route)  37.1 us
    ppermute x20, waiting for transfers between devices, meet(): return lax.ppermute(x, ('section', axis), route)  29.6 us
    pallas_call x6, Pallas kernels, relay(): pl.pallas_call(functools.partial(relay_kernel, first, who), in_specs=spec...  24.5 us
    pallas_call x2, Pallas kernels, forward(): pl.pallas_call(functools.partial(forward_kernel, m), in_specs=[SMEM, HBM,...  16.9 us
    pallas_call x2, Pallas kernels, tap_terms(): pl.pallas_call(functools.partial(tap_kernel, m), in_specs=[SMEM, HBM, HBM...  11.4 us
    pallas_call x1, Pallas kernels, weight_terms(): pl.pallas_call(weight_kernel, in_specs=[SMEM, ANY, ANY, HBM] + [ANY] * le...  11.3 us
    ppermute x4, starting transfers between devices, swap(): return lax.ppermute(x, axis, [(i, i ^ d) for i in range(n)])  9.23 us
  transfers between devices with their start and end apart: 30, of which 20 were waited for; matrix products, arithmetic and copies ran while one was open for 2% of the time, Pallas kernels for 19%

profile of v1, /device:TPU:0, one launch (start us, length us, event | category | flops | bytes accessed | tf_op | source)
XLA Modules:
  0.0 218.8 jit_solution(15817255143066374237)
XLA Ops:
  2.5 3.2 %collective-permute-start = (bf16[64,768]{1,0:T(8,128)(2,1)S(1)}, bf16[64,768]{1,0:T(8,128)(2,1)S(1)}, u32[]{:S(2)}, u32[]{:S(2)}) collective-permute-start(bf16[64,768]{1,0:T(8,128)(2,1)S(1)} %get-tuple-element.120), channel_id=1, source_target_pairs={{0,16},{16,0},{1,17},{17,1},{2,18},{18,2},{3,19},{19,3},{4,20},{20... | collective-permute-start | bytes 294920 | tf_op jit(solution)/shard_map/ppermute | solution.py:548
  6.1 2.6 %collective-permute-done = bf16[64,768]{1,0:T(8,128)(2,1)S(1)} collective-permute-done((bf16[64,768]{1,0:T(8,128)(2,1)S(1)}, bf16[64,768]{1,0:T(8,128)(2,1)S(1)}, u32[]{:S(2)}, u32[]{:S(2)}) %collective-permute-start) | collective-permute-done | bytes 98336 | tf_op jit(solution)/shard_map/ppermute | solution.py:548
  14.5 3.3 %collective-permute-start.2 = (bf16[4,64,768]{2,1,0:T(8,128)(2,1)S(1)}, bf16[4,64,768]{2,1,0:T(8,128)(2,1)S(1)}, u32[]{:S(2)}, u32[]{:S(2)}) collective-permute-start(bf16[4,64,768]{2,1,0:T(8,128)(2,1)S(1)} %pad_maximum_fusion.5), channel_id=1, source_target_pairs={{0,3},{1,2},{2,1},{3,0},{32,33},{33,32},{34,35},{35,34},{64,67},{6... | collective-permute-start | bytes 1179656 | tf_op jit(solution)/shard_map/ppermute | solution.py:558
  17.8 4.1 %collective-permute-start.7 = (bf16[4,48,768]{2,1,0:T(8,128)(2,1)S(1)}, bf16[4,48,768]{2,1,0:T(8,128)(2,1)S(1)}, u32[]{:S(2)}, u32[]{:S(2)}) collective-permute-start(bf16[4,48,768]{2,1,0:T(8,128)(2,1)S(1)} %pad_maximum_fusion.6), channel_id=1, source_target_pairs={{0,12},{4,8},{8,4},{12,0},{32,36},{36,32},{40,44},{44,40},{64,76},... | collective-permute-start | bytes 884744 | tf_op jit(solution)/shard_map/ppermute | solution.py:558
  27.6 4.2 %collective-permute-start.4 = (bf16[16,768]{1,0:T(8,128)(2,1)S(1)}, bf16[16,768]{1,0:T(8,128)(2,1)S(1)}, u32[]{:S(2)}, u32[]{:S(2)}) collective-permute-start(bf16[16,768]{1,0:T(8,128)(2,1)S(1)} %add.82), channel_id=1, source_target_pairs={{0,12},{4,8},{8,4},{12,0},{32,36},{36,32},{40,44},{44,40},{64,76},... | collective-permute-start | bytes 73736 | tf_op jit(solution)/shard_map/ppermute | solution.py:558
  35.1 8.4 %shard_map.102 = (bf16[512,1536]{1,0:T(8,128)(2,1)}, bf16[512,1536]{1,0:T(8,128)(2,1)}, f32[512,128]{1,0:T(8,128)}, bf16[1536,512]{1,0:T(8,128)(2,1)}) custom-call(s32[2]{0:T(128)} %bitcast.54, bf16[2,512,1536]{2,1,0:T(8,128)(2,1)} %bitcast.57, f32[8,1536]{1,0:T(8,128)} %maximum_convert_fusion.taps.rest_10_), custom_call_target="tpu_custom_call" | custom-call | flops 8000000000 | bytes 1048576 | tf_op jit(solution)/shard_map/pallas_call | solution.py:149
  45.2 3.1 %collective-permute-start.11 = (bf16[16,48,768]{2,1,0:T(8,128)(2,1)S(1)}, bf16[16,48,768]{2,1,0:T(8,128)(2,1)S(1)}, u32[]{:S(2)}, u32[]{:S(2)}) collective-permute-start(bf16[16,48,768]{2,1,0:T(8,128)(2,1)S(1)} %constant_dynamic-update-slice_fusion.2.rest_2_), channel_id=1, source_target_pairs={{0,3},{1,2},{2,1},{3,0},{32,33},{33,32},{34,35},{35,34},{64,67},{6... | collective-permute-start | bytes 3538952 | tf_op jit(solution)/shard_map/ppermute | solution.py:558
  49.4 4.4 %collective-permute-start.10 = (bf16[16,48,768]{2,1,0:T(8,128)(2,1)S(1)}, bf16[16,48,768]{2,1,0:T(8,128)(2,1)}, u32[]{:S(2)}, u32[]{:S(2)}) collective-permute-start(bf16[16,48,768]{2,1,0:T(8,128)(2,1)S(1)} %constant_dynamic-update-slice_fusion.rest_0_), channel_id=1, source_target_pairs={{0,12},{4,8},{8,4},{12,0},{32,36},{36,32},{40,44},{44,40},{64,76},... | collective-permute-start | bytes 3538952 | tf_op jit(solution)/shard_map/ppermute | solution.py:558
  55.2 8.5 %shard_map.103 = (bf16[512,1536]{1,0:T(8,128)(2,1)}, bf16[512,1536]{1,0:T(8,128)(2,1)}, f32[512,128]{1,0:T(8,128)}, bf16[1536,512]{1,0:T(8,128)(2,1)}) custom-call(s32[2]{0:T(128)} %bitcast.55, bf16[2,512,1536]{2,1,0:T(8,128)(2,1)} %bitcast.58, f32[8,1536]{1,0:T(8,128)} %maximum_convert_fusion.taps.rest_10_), custom_call_target="tpu_custom_call" | custom-call | flops 8000000000 | bytes 1048576 | tf_op jit(solution)/shard_map/pallas_call | solution.py:149
  63.7 4.4 %collective-permute-done.10.rest_1_ = bf16[16,48,768]{2,1,0:T(8,128)(2,1)} collective-permute-done((bf16[16,48,768]{2,1,0:T(8,128)(2,1)S(1)}, bf16[16,48,768]{2,1,0:T(8,128)(2,1)}, u32[]{:S(2)}, u32[]{:S(2)}) %collective-permute-start.10) | collective-permute-done | bytes 1179680 | tf_op jit(solution)/shard_map/ppermute | solution.py:558
  81.1 45.0 %collective-permute-done.15.come.rest_1_ = bf16[512,1536]{1,0:T(8,128)(2,1)S(1)} collective-permute-done((bf16[512,1536]{1,0:T(8,128)(2,1)}, bf16[512,1536]{1,0:T(8,128)(2,1)S(1)}, u32[]{:S(2)}, u32[]{:S(2)}) %collective-permute-start.15) | collective-permute-done | bytes 1572896 | tf_op jit(solution)/shard_map/ppermute | solution.py:638
  127.2 10.3 %shard_map.109 = (bf16[512,1536]{1,0:T(8,128)(2,1)}, bf16[2,512,1536]{2,1,0:T(8,128)(2,1)}, f32[2,8,1536]{2,1,0:T(8,128)}) custom-call(s32[136]{0:T(256)} %concatenate.57.meta, bf16[2,512,1536]{2,1,0:T(8,128)(2,1)} %bitcast.42, bf16[512,1536]{1,0:T(8,128)(2,1)} %copy-done.7, ...), custom_call_target="tpu_custom_call", output_to_operand_aliasing={{1}: (15, {}), {2}: (16, {})} | custom-call | flops 1000000000 | bytes 1048576 | tf_op jit(solution)/shard_map/pallas_call | solution.py:342
  138.8 5.1 %shard_map.110 = f32[8,1536]{1,0:T(8,128)} custom-call(s32[136]{0:T(256)} %concatenate.57.meta, bf16[2,512,1536]{2,1,0:T(8,128)(2,1)} %bitcast.59, bf16[2,512,1536]{2,1,0:T(8,128)(2,1)} %get-tuple-element.86.mixed_in.rest_11_, f32[2,8,1536]{2,1,0:T(8,128)} %get-tuple-element.87.gain_in.rest_12_, f32[8,1536]{1,0:T(8,128)} %maximum_convert_fusion.taps.rest_10_), custom_call_target="tpu_custom_call" | custom-call | flops 5000000000 | bytes 1048576 | tf_op jit(solution)/shard_map/pallas_call | solution.py:514
  145.2 11.3 %shard_map.113 = (bf16[16,48,768]{2,1,0:T(8,128)(2,1)}, bf16[16,48,768]{2,1,0:T(8,128)(2,1)}, bf16[16,48,768]{2,1,0:T(8,128)(2,1)}, bf16[16,48,768]{2,1,0:T(8,128)(2,1)}) custom-call(s32[136]{0:T(256)} %concatenate.57.meta, bf16[1536,512]{1,0:T(8,128)(2,1)} %get-tuple-element.93.act_a, bf16[1536,512]{1,0:T(8,128)(2,1)} %get-tuple-element.94.act_b, ...), custom_call_target="tpu_custom_call" | custom-call | flops 8000000000 | bytes 1048576 | tf_op jit(solution)/shard_map/pallas_call | solution.py:424
  156.5 3.2 %collective-permute-start.18 = (bf16[16,48,768]{2,1,0:T(8,128)(2,1)}, bf16[16,48,768]{2,1,0:T(8,128)(2,1)S(1)}, u32[]{:S(2)}, u32[]{:S(2)}) collective-permute-start(bf16[16,48,768]{2,1,0:T(8,128)(2,1)} %get-tuple-element.96), channel_id=1, source_target_pairs={{0,4},{4,0},{8,12},{12,8},{32,44},{36,40},{40,36},{44,32},{64,68},... | collective-permute-start | bytes 3538952 | tf_op jit(solution)/shard_map/ppermute | solution.py:558
  159.7 10.5 %shard_map.111 = (bf16[512,1536]{1,0:T(8,128)(2,1)}, bf16[2,512,1536]{2,1,0:T(8,128)(2,1)}, f32[2,8,1536]{2,1,0:T(8,128)}) custom-call(s32[136]{0:T(256)} %concatenate.57.meta, bf16[2,512,1536]{2,1,0:T(8,128)(2,1)} %bitcast.44, bf16[512,1536]{1,0:T(8,128)(2,1)} %copy-done.6, ...), custom_call_target="tpu_custom_call", output_to_operand_aliasing={{1}: (15, {}), {2}: (16, {})} | custom-call | flops 1000000000 | bytes 1048576 | tf_op jit(solution)/shard_map/pallas_call | solution.py:342
  170.2 6.2 %shard_map.112 = (f32[8,1536]{1,0:T(8,128)}, bf16[2,512,1536]{2,1,0:T(8,128)(2,1)}) custom-call(s32[136]{0:T(256)} %concatenate.57.meta, bf16[2,512,1536]{2,1,0:T(8,128)(2,1)} %bitcast.60, bf16[2,512,1536]{2,1,0:T(8,128)(2,1)} %get-tuple-element.89.mixed_in, f32[2,8,1536]{2,1,0:T(8,128)} %get-tuple-element.90.gain_in, ...), custom_call_target="tpu_custom_call" | custom-call | flops 5000000000 | bytes 1048576 | tf_op jit(solution)/shard_map/pallas_call | solution.py:514
  179.5 2.7 %collective-permute-start.22 = (bf16[8,48,768]{2,1,0:T(8,128)(2,1)S(1)}, bf16[8,48,768]{2,1,0:T(8,128)(2,1)S(1)}, u32[]{:S(2)}, u32[]{:S(2)}) collective-permute-start(bf16[8,48,768]{2,1,0:T(8,128)(2,1)S(1)} %slice.194), channel_id=1, source_target_pairs={{0,12},{4,8},{8,4},{12,0},{32,36},{36,32},{40,44},{44,40},{64,76},... | collective-permute-start | bytes 1769480 | tf_op jit(solution)/shard_map/ppermute | solution.py:558
  183.2 4.7 %collective-permute-done.20 = f32[16,768]{1,0:T(8,128)S(1)} collective-permute-done((f32[16,768]{1,0:T(8,128)S(1)}, f32[16,768]{1,0:T(8,128)S(1)}, u32[]{:S(2)}, u32[]{:S(2)}) %collective-permute-start.20) | collective-permute-done | bytes 49184 | tf_op jit(solution)/shard_map/ppermute | solution.py:558
  188.0 5.2 %collective-permute-done.21 = f32[16,768]{1,0:T(8,128)S(1)} collective-permute-done((f32[16,768]{1,0:T(8,128)S(1)}, f32[16,768]{1,0:T(8,128)S(1)}, u32[]{:S(2)}, u32[]{:S(2)}) %collective-permute-start.21) | collective-permute-done | bytes 49184 | tf_op jit(solution)/shard_map/ppermute | solution.py:558
  194.7 5.6 %collective-permute-done.27 = bf16[4,48,768]{2,1,0:T(8,128)(2,1)S(1)} collective-permute-done((bf16[4,48,768]{2,1,0:T(8,128)(2,1)S(1)}, bf16[4,48,768]{2,1,0:T(8,128)(2,1)S(1)}, u32[]{:S(2)}, u32[]{:S(2)}) %collective-permute-start.27) | collective-permute-done | bytes 294944 | tf_op jit(solution)/shard_map/ppermute | solution.py:558
  204.0 2.7 %collective-permute-done.28 = bf16[2,48,768]{2,1,0:T(8,128)(2,1)S(1)} collective-permute-done((bf16[2,48,768]{2,1,0:T(8,128)(2,1)S(1)}, bf16[2,48,768]{2,1,0:T(8,128)(2,1)S(1)}, u32[]{:S(2)}, u32[]{:S(2)}) %collective-permute-start.28) | collective-permute-done | bytes 147488 | tf_op jit(solution)/shard_map/ppermute | solution.py:558
  206.8 3.8 %collective-permute-start.29 = (bf16[48,768]{1,0:T(8,128)(2,1)S(1)}, bf16[48,768]{1,0:T(8,128)(2,1)S(1)}, u32[]{:S(2)}, u32[]{:S(2)}) collective-permute-start(bf16[48,768]{1,0:T(8,128)(2,1)S(1)} %fusion.7), channel_id=1, source_target_pairs={{0,16},{16,0},{1,17},{17,1},{2,18},{18,2},{3,19},{19,3},{4,20},{20... | collective-permute-start | bytes 221192 | tf_op jit(solution)/shard_map/ppermute | solution.py:548
  212.9 3.9 %collective-permute-done.26 = bf16[64,768]{1,0:T(8,128)(2,1)S(1)} collective-permute-done((bf16[64,768]{1,0:T(8,128)(2,1)S(1)}, bf16[64,768]{1,0:T(8,128)(2,1)S(1)}, u32[]{:S(2)}, u32[]{:S(2)}) %collective-permute-start.26) | collective-permute-done | bytes 98336 | tf_op jit(solution)/shard_map/ppermute | solution.py:548
  (128 shorter events, 51.2 us)
Async XLA Ops:
  2.5 6.2 %collective-permute-start = (bf16[64,768]{1,0:T(8,128)(2,1)S(1)}, bf16[64,768]{1,0:T(8,128)(2,1)S(1)}, u32[]{:S(2)}, u32[]{:S(2)}) collective-permute-start(bf16[64,768]{1,0:T(8,128)(2,1)S(1)} %get-tuple-element.120), channel_id=1, source_target_pairs={{0,16},{16,0},{1,17},{17,1},{2,18},{18,2},{3,19},{19,3},{4,20},{20... | collective-permute-start | bytes 294920 | tf_op jit(solution)/shard_map/ppermute | solution.py:548
  5.7 5.9 %collective-permute-start.5 = (bf16[48,768]{1,0:T(8,128)(2,1)S(1)}, bf16[48,768]{1,0:T(8,128)(2,1)S(1)}, u32[]{:S(2)}, u32[]{:S(2)}) collective-permute-start(bf16[48,768]{1,0:T(8,128)(2,1)S(1)} %get-tuple-element.117), channel_id=1, source_target_pairs={{0,16},{16,0},{1,17},{17,1},{2,18},{18,2},{3,19},{19,3},{4,20},{20... | collective-permute-start | bytes 221192 | tf_op jit(solution)/shard_map/ppermute | solution.py:548
  8.7 5.7 %collective-permute-start.1 = (bf16[2,64,768]{2,1,0:T(8,128)(2,1)S(1)}, bf16[2,64,768]{2,1,0:T(8,128)(2,1)S(1)}, u32[]{:S(2)}, u32[]{:S(2)}) collective-permute-start(bf16[2,64,768]{2,1,0:T(8,128)(2,1)S(1)} %pad_maximum_fusion.7), channel_id=1, source_target_pairs={{0,1},{1,0},{2,3},{3,2},{32,35},{33,34},{34,33},{35,32},{64,65},{6... | collective-permute-start | bytes 589832 | tf_op jit(solution)/shard_map/ppermute | solution.py:558
  11.6 6.2 %collective-permute-start.6 = (bf16[2,48,768]{2,1,0:T(8,128)(2,1)S(1)}, bf16[2,48,768]{2,1,0:T(8,128)(2,1)S(1)}, u32[]{:S(2)}, u32[]{:S(2)}) collective-permute-start(bf16[2,48,768]{2,1,0:T(8,128)(2,1)S(1)} %pad_maximum_fusion.8), channel_id=1, source_target_pairs={{0,4},{4,0},{8,12},{12,8},{32,44},{36,40},{40,36},{44,32},{64,68},... | collective-permute-start | bytes 442376 | tf_op jit(solution)/shard_map/ppermute | solution.py:558
  14.5 9.1 %collective-permute-start.2 = (bf16[4,64,768]{2,1,0:T(8,128)(2,1)S(1)}, bf16[4,64,768]{2,1,0:T(8,128)(2,1)S(1)}, u32[]{:S(2)}, u32[]{:S(2)}) collective-permute-start(bf16[4,64,768]{2,1,0:T(8,128)(2,1)S(1)} %pad_maximum_fusion.5), channel_id=1, source_target_pairs={{0,3},{1,2},{2,1},{3,0},{32,33},{33,32},{34,35},{35,34},{64,67},{6... | collective-permute-start | bytes 1179656 | tf_op jit(solution)/shard_map/ppermute | solution.py:558
  17.8 9.1 %collective-permute-start.7 = (bf16[4,48,768]{2,1,0:T(8,128)(2,1)S(1)}, bf16[4,48,768]{2,1,0:T(8,128)(2,1)S(1)}, u32[]{:S(2)}, u32[]{:S(2)}) collective-permute-start(bf16[4,48,768]{2,1,0:T(8,128)(2,1)S(1)} %pad_maximum_fusion.6), channel_id=1, source_target_pairs={{0,12},{4,8},{8,4},{12,0},{32,36},{36,32},{40,44},{44,40},{64,76},... | collective-permute-start | bytes 884744 | tf_op jit(solution)/shard_map/ppermute | solution.py:558
  27.6 6.2 %collective-permute-start.4 = (bf16[16,768]{1,0:T(8,128)(2,1)S(1)}, bf16[16,768]{1,0:T(8,128)(2,1)S(1)}, u32[]{:S(2)}, u32[]{:S(2)}) collective-permute-start(bf16[16,768]{1,0:T(8,128)(2,1)S(1)} %add.82), channel_id=1, source_target_pairs={{0,12},{4,8},{8,4},{12,0},{32,36},{36,32},{40,44},{44,40},{64,76},... | collective-permute-start | bytes 73736 | tf_op jit(solution)/shard_map/ppermute | solution.py:558
  33.8 10.1 %collective-permute-start.8 = (bf16[8,48,768]{2,1,0:T(8,128)(2,1)S(1)}, bf16[8,48,768]{2,1,0:T(8,128)(2,1)}, u32[]{:S(2)}, u32[]{:S(2)}) collective-permute-start(bf16[8,48,768]{2,1,0:T(8,128)(2,1)S(1)} %pad_maximum_fusion.1), channel_id=1, source_target_pairs={{0,4},{4,0},{8,12},{12,8},{32,44},{36,40},{40,36},{44,32},{64,68},... | collective-permute-start | bytes 1769480 | tf_op jit(solution)/shard_map/ppermute | solution.py:558
  34.0 10.1 %collective-permute-start.9 = (bf16[8,48,768]{2,1,0:T(8,128)(2,1)S(1)}, bf16[8,48,768]{2,1,0:T(8,128)(2,1)}, u32[]{:S(2)}, u32[]{:S(2)}) collective-permute-start(bf16[8,48,768]{2,1,0:T(8,128)(2,1)S(1)} %pad_maximum_fusion.4), channel_id=1, source_target_pairs={{0,1},{1,0},{2,3},{3,2},{32,35},{33,34},{34,33},{35,32},{64,65},{6... | collective-permute-start | bytes 1769480 | tf_op jit(solution)/shard_map/ppermute | solution.py:558
  45.2 18.5 %collective-permute-start.11 = (bf16[16,48,768]{2,1,0:T(8,128)(2,1)S(1)}, bf16[16,48,768]{2,1,0:T(8,128)(2,1)S(1)}, u32[]{:S(2)}, u32[]{:S(2)}) collective-permute-start(bf16[16,48,768]{2,1,0:T(8,128)(2,1)S(1)} %constant_dynamic-update-slice_fusion.2.rest_2_), channel_id=1, source_target_pairs={{0,3},{1,2},{2,1},{3,0},{32,33},{33,32},{34,35},{35,34},{64,67},{6... | collective-permute-start | bytes 3538952 | tf_op jit(solution)/shard_map/ppermute | solution.py:558
  49.4 18.7 %collective-permute-start.10 = (bf16[16,48,768]{2,1,0:T(8,128)(2,1)S(1)}, bf16[16,48,768]{2,1,0:T(8,128)(2,1)}, u32[]{:S(2)}, u32[]{:S(2)}) collective-permute-start(bf16[16,48,768]{2,1,0:T(8,128)(2,1)S(1)} %constant_dynamic-update-slice_fusion.rest_0_), channel_id=1, source_target_pairs={{0,12},{4,8},{8,4},{12,0},{32,36},{36,32},{40,44},{44,40},{64,76},... | collective-permute-start | bytes 3538952 | tf_op jit(solution)/shard_map/ppermute | solution.py:558
  78.6 47.4 %collective-permute-start.15 = (bf16[512,1536]{1,0:T(8,128)(2,1)}, bf16[512,1536]{1,0:T(8,128)(2,1)S(1)}, u32[]{:S(2)}, u32[]{:S(2)}) collective-permute-start(bf16[512,1536]{1,0:T(8,128)(2,1)} %get-tuple-element.81.rest_3_), channel_id=1, source_target_pairs={{32,0},{33,1},{34,2},{35,3},{36,4},{37,5},{38,6},{39,7},{40,8},{41... | collective-permute-start | bytes 4718600 | tf_op jit(solution)/shard_map/ppermute | solution.py:638
  137.5 6.5 %collective-permute-start.17 = (bf16[512,1536]{1,0:T(8,128)(2,1)}, bf16[512,1536]{1,0:T(8,128)(2,1)S(1)}, u32[]{:S(2)}, u32[]{:S(2)}) collective-permute-start(bf16[512,1536]{1,0:T(8,128)(2,1)} %get-tuple-element.85.rest_4_), channel_id=1, source_target_pairs={{32,0},{33,1},{34,2},{35,3},{36,4},{37,5},{38,6},{39,7},{40,8},{41... | collective-permute-start | bytes 4718600 | tf_op jit(solution)/shard_map/ppermute | solution.py:638
  156.5 20.8 %collective-permute-start.18 = (bf16[16,48,768]{2,1,0:T(8,128)(2,1)}, bf16[16,48,768]{2,1,0:T(8,128)(2,1)S(1)}, u32[]{:S(2)}, u32[]{:S(2)}) collective-permute-start(bf16[16,48,768]{2,1,0:T(8,128)(2,1)} %get-tuple-element.96), channel_id=1, source_target_pairs={{0,4},{4,0},{8,12},{12,8},{32,44},{36,40},{40,36},{44,32},{64,68},... | collective-permute-start | bytes 3538952 | tf_op jit(solution)/shard_map/ppermute | solution.py:558
  159.7 17.6 %collective-permute-start.19 = (bf16[16,48,768]{2,1,0:T(8,128)(2,1)}, bf16[16,48,768]{2,1,0:T(8,128)(2,1)}, u32[]{:S(2)}, u32[]{:S(2)}) collective-permute-start(bf16[16,48,768]{2,1,0:T(8,128)(2,1)} %get-tuple-element.97), channel_id=1, source_target_pairs={{0,1},{1,0},{2,3},{3,2},{32,35},{33,34},{34,33},{35,32},{64,65},{6... | collective-permute-start | bytes 3538952 | tf_op jit(solution)/shard_map/ppermute | solution.py:558
  179.5 13.7 %collective-permute-start.22 = (bf16[8,48,768]{2,1,0:T(8,128)(2,1)S(1)}, bf16[8,48,768]{2,1,0:T(8,128)(2,1)S(1)}, u32[]{:S(2)}, u32[]{:S(2)}) collective-permute-start(bf16[8,48,768]{2,1,0:T(8,128)(2,1)S(1)} %slice.194), channel_id=1, source_target_pairs={{0,12},{4,8},{8,4},{12,0},{32,36},{36,32},{40,44},{44,40},{64,76},... | collective-permute-start | bytes 1769480 | tf_op jit(solution)/shard_map/ppermute | solution.py:558
  182.2 11.1 %collective-permute-start.23 = (bf16[8,48,768]{2,1,0:T(8,128)(2,1)S(1)}, bf16[8,48,768]{2,1,0:T(8,128)(2,1)S(1)}, u32[]{:S(2)}, u32[]{:S(2)}) collective-permute-start(bf16[8,48,768]{2,1,0:T(8,128)(2,1)S(1)} %slice.193), channel_id=1, source_target_pairs={{0,3},{1,2},{2,1},{3,0},{32,33},{33,32},{34,35},{35,34},{64,67},{6... | collective-permute-start | bytes 1769480 | tf_op jit(solution)/shard_map/ppermute | solution.py:558
  187.8 5.4 %collective-permute-start.21 = (f32[16,768]{1,0:T(8,128)S(1)}, f32[16,768]{1,0:T(8,128)S(1)}, u32[]{:S(2)}, u32[]{:S(2)}) collective-permute-start(f32[16,768]{1,0:T(8,128)S(1)} %add.87), channel_id=1, source_target_pairs={{0,12},{4,8},{8,4},{12,0},{32,36},{36,32},{40,44},{44,40},{64,76},... | collective-permute-start | bytes 147464 | tf_op jit(solution)/shard_map/ppermute | solution.py:558
  193.5 6.8 %collective-permute-start.27 = (bf16[4,48,768]{2,1,0:T(8,128)(2,1)S(1)}, bf16[4,48,768]{2,1,0:T(8,128)(2,1)S(1)}, u32[]{:S(2)}, u32[]{:S(2)}) collective-permute-start(bf16[4,48,768]{2,1,0:T(8,128)(2,1)S(1)} %slice.195), channel_id=1, source_target_pairs={{0,4},{4,0},{8,12},{12,8},{32,44},{36,40},{40,36},{44,32},{64,68},... | collective-permute-start | bytes 884744 | tf_op jit(solution)/shard_map/ppermute | solution.py:558
  193.8 7.9 %collective-permute-start.24 = (bf16[4,64,768]{2,1,0:T(8,128)(2,1)S(1)}, bf16[4,64,768]{2,1,0:T(8,128)(2,1)S(1)}, u32[]{:S(2)}, u32[]{:S(2)}) collective-permute-start(bf16[4,64,768]{2,1,0:T(8,128)(2,1)S(1)} %fusion.2), channel_id=1, source_target_pairs={{0,1},{1,0},{2,3},{3,2},{32,35},{33,34},{34,33},{35,32},{64,65},{6... | collective-permute-start | bytes 1179656 | tf_op jit(solution)/shard_map/ppermute | solution.py:558
  200.3 6.4 %collective-permute-start.28 = (bf16[2,48,768]{2,1,0:T(8,128)(2,1)S(1)}, bf16[2,48,768]{2,1,0:T(8,128)(2,1)S(1)}, u32[]{:S(2)}, u32[]{:S(2)}) collective-permute-start(bf16[2,48,768]{2,1,0:T(8,128)(2,1)S(1)} %slice.197), channel_id=1, source_target_pairs={{0,12},{4,8},{8,4},{12,0},{32,36},{36,32},{40,44},{44,40},{64,76},... | collective-permute-start | bytes 442376 | tf_op jit(solution)/shard_map/ppermute | solution.py:558
  201.7 8.9 %collective-permute-start.25 = (bf16[2,64,768]{2,1,0:T(8,128)(2,1)S(1)}, bf16[2,64,768]{2,1,0:T(8,128)(2,1)S(1)}, u32[]{:S(2)}, u32[]{:S(2)}) collective-permute-start(bf16[2,64,768]{2,1,0:T(8,128)(2,1)S(1)} %slice.196), channel_id=1, source_target_pairs={{0,3},{1,2},{2,1},{3,0},{32,33},{33,32},{34,35},{35,34},{64,67},{6... | collective-permute-start | bytes 589832 | tf_op jit(solution)/shard_map/ppermute | solution.py:558
  206.8 6.1 %collective-permute-start.29 = (bf16[48,768]{1,0:T(8,128)(2,1)S(1)}, bf16[48,768]{1,0:T(8,128)(2,1)S(1)}, u32[]{:S(2)}, u32[]{:S(2)}) collective-permute-start(bf16[48,768]{1,0:T(8,128)(2,1)S(1)} %fusion.7), channel_id=1, source_target_pairs={{0,16},{16,0},{1,17},{17,1},{2,18},{18,2},{3,19},{19,3},{4,20},{20... | collective-permute-start | bytes 221192 | tf_op jit(solution)/shard_map/ppermute | solution.py:548
  210.7 6.2 %collective-permute-start.26 = (bf16[64,768]{1,0:T(8,128)(2,1)S(1)}, bf16[64,768]{1,0:T(8,128)(2,1)S(1)}, u32[]{:S(2)}, u32[]{:S(2)}) collective-permute-start(bf16[64,768]{1,0:T(8,128)(2,1)S(1)} %fusion.6), channel_id=1, source_target_pairs={{0,16},{16,0},{1,17},{17,1},{2,18},{18,2},{3,19},{19,3},{4,20},{20... | collective-permute-start | bytes 294920 | tf_op jit(solution)/shard_map/ppermute | solution.py:548
  (19 other events, 94.2 us)

commit v2 on v1

--- a/solution.py
+++ b/solution.py
@@ -175,7 +175,7 @@
 
 
 def relay_kernel(first, who, meta, grads, come, come_one, *rest):
-    (wa, wb), rest = (rest[:2], rest[2:4]), rest[4:]
+    (wa, wb), rest = (rest[:4], rest[4:8]), rest[8:]
     (normed_in, slope_in, inv_in), taps, rest = (rest[0:2], rest[2:4], rest[4:6]), rest[6], rest[7:]
     if not first:
         rest = rest[2:]
@@ -194,9 +194,9 @@
         made = []
         odd = (place_x + group) % 2
         for h, parts in enumerate((wa, wb)):
-            for p in range(2):
-                for j in range(8):
-                    at = h * 32 + p * 16 + 2 * j + odd
+            for p in range(4):
+                for j in range(4):
+                    at = h * 32 + p * 8 + 2 * j + odd
                     place = pl.multiple_of(meta[8 + at] * rows, 16)
                     made.append(
                         pltpu.make_async_copy(
@@ -575,9 +575,11 @@
     come = [meet(p, a, 0) for p, a in zip(pieces, axes[::-1])]
     whole = jnp.concatenate([small[:8], small[8:]], axis=1).astype(F32)
     made = [run(0, whole)]
+    far = [meet(p, a, 1) for p, a in zip(pieces, axes[::-1])]
     made, come, whole = lax.optimization_barrier((made, come, whole))
-    pieces = [jnp.concatenate([p, c]) for p, c in zip(pieces, come)]
-    pieces = [(p, meet(p, a, 1)) for p, a in zip(pieces, axes[::-1])]
+    pieces = [
+        (p, c, f, meet(c, a, 1)) for p, c, f, a in zip(pieces, come, far, axes[::-1])
+    ]
     made.append(run(1, whole))
     return [*pieces[0], *pieces[1]], whole, made
 

time: 220 us -> 216 us (0.982)
  starting transfers between devices: 52.1 us -> 49.1 us
    ppermute x20 -> x22, starting transfers between devices: 37.1 us -> 34.7 us  [meet(): return lax.ppermute(x, ('section', axis), route)]
    concatenate x2 -> x0, local copies, waits for them, and re-layouts: 2.22 us -> none  [gather_weights(): pieces = [jnp.concatenate([p, c]) for p, c in zip(pieces, come)]]
    unnamed x29 -> x35, local copies, waits for them, and re-layouts: 7.64 us -> 8.29 us
    ppermute x20 -> x22, waiting for transfers between devices: 29.6 us -> 30.3 us  [meet(): return lax.ppermute(x, ('section', axis), route)]
  transfers between devices with their start and end apart: 30 -> 32, of which waited for: 20 -> 18; matrix products, arithmetic and copies ran while one was open for 2% -> 2% of each run, Pallas kernels for 19% -> 19%
where the time goes in v2:
time: 216 us; the launch traced here: 215 us
  waiting for transfers between devices  83.1 us (38%)
  Pallas kernels  64 us (30%)
  starting transfers between devices  49.1 us (23%)
  local copies, waits for them, and re-layouts  11.5 us (5%)
  other arithmetic  5.71 us (3%)
    ppermute x6, waiting for transfers between devices, hop(): return lax.ppermute(block, 'section', [(source, source - 1)])  44.9 us
    ppermute x22, starting transfers between devices, meet(): return lax.ppermute(x, ('section', axis), route)  34.7 us
    ppermute x22, waiting for transfers between devices, meet(): return lax.ppermute(x, ('section', axis), route)  30.3 us
    pallas_call x6, Pallas kernels, relay(): pl.pallas_call(functools.partial(relay_kernel, first, who), in_specs=spec...  24.4 us
    pallas_call x2, Pallas kernels, forward(): pl.pallas_call(functools.partial(forward_kernel, m), in_specs=[SMEM, HBM,...  16.9 us
    pallas_call x2, Pallas kernels, tap_terms(): pl.pallas_call(functools.partial(tap_kernel, m), in_specs=[SMEM, HBM, HBM...  11.4 us
    pallas_call x1, Pallas kernels, weight_terms(): pl.pallas_call(weight_kernel, in_specs=[SMEM, ANY, ANY, HBM] + [ANY] * le...  11.3 us
    ppermute x4, starting transfers between devices, swap(): return lax.ppermute(x, axis, [(i, i ^ d) for i in range(n)])  8.56 us
  transfers between devices with their start and end apart: 32, of which 18 were waited for; matrix products, arithmetic and copies ran while one was open for 2% of the time, Pallas kernels for 19%

profile of v2, /device:TPU:0, one launch (start us, length us, event | category | flops | bytes accessed | tf_op | source)
XLA Modules:
  0.0 214.7 jit_solution(8782644216858404344)
XLA Ops:
  2.5 3.2 %collective-permute-start = (bf16[64,768]{1,0:T(8,128)(2,1)S(1)}, bf16[64,768]{1,0:T(8,128)(2,1)S(1)}, u32[]{:S(2)}, u32[]{:S(2)}) collective-permute-start(bf16[64,768]{1,0:T(8,128)(2,1)S(1)} %get-tuple-element.120), channel_id=1, source_target_pairs={{0,16},{16,0},{1,17},{17,1},{2,18},{18,2},{3,19},{19,3},{4,20},{20... | collective-permute-start | bytes 294920 | tf_op jit(solution)/shard_map/ppermute | solution.py:548
  6.1 2.6 %collective-permute-done = bf16[64,768]{1,0:T(8,128)(2,1)S(1)} collective-permute-done((bf16[64,768]{1,0:T(8,128)(2,1)S(1)}, bf16[64,768]{1,0:T(8,128)(2,1)S(1)}, u32[]{:S(2)}, u32[]{:S(2)}) %collective-permute-start) | collective-permute-done | bytes 98336 | tf_op jit(solution)/shard_map/ppermute | solution.py:548
  14.5 3.3 %collective-permute-start.2 = (bf16[4,64,768]{2,1,0:T(8,128)(2,1)S(1)}, bf16[4,64,768]{2,1,0:T(8,128)(2,1)S(1)}, u32[]{:S(2)}, u32[]{:S(2)}) collective-permute-start(bf16[4,64,768]{2,1,0:T(8,128)(2,1)S(1)} %pad_maximum_fusion.5), channel_id=1, source_target_pairs={{0,3},{1,2},{2,1},{3,0},{32,33},{33,32},{34,35},{35,34},{64,67},{6... | collective-permute-start | bytes 1179656 | tf_op jit(solution)/shard_map/ppermute | solution.py:558
  17.8 4.1 %collective-permute-start.7 = (bf16[4,48,768]{2,1,0:T(8,128)(2,1)S(1)}, bf16[4,48,768]{2,1,0:T(8,128)(2,1)S(1)}, u32[]{:S(2)}, u32[]{:S(2)}) collective-permute-start(bf16[4,48,768]{2,1,0:T(8,128)(2,1)S(1)} %pad_maximum_fusion.6), channel_id=1, source_target_pairs={{0,12},{4,8},{8,4},{12,0},{32,36},{36,32},{40,44},{44,40},{64,76},... | collective-permute-start | bytes 884744 | tf_op jit(solution)/shard_map/ppermute | solution.py:558
  27.6 4.2 %collective-permute-start.4 = (bf16[16,768]{1,0:T(8,128)(2,1)S(1)}, bf16[16,768]{1,0:T(8,128)(2,1)S(1)}, u32[]{:S(2)}, u32[]{:S(2)}) collective-permute-start(bf16[16,768]{1,0:T(8,128)(2,1)S(1)} %add.82), channel_id=1, source_target_pairs={{0,12},{4,8},{8,4},{12,0},{32,36},{36,32},{40,44},{44,40},{64,76},... | collective-permute-start | bytes 73736 | tf_op jit(solution)/shard_map/ppermute | solution.py:558
  33.9 3.3 %collective-permute-start.10 = (bf16[8,48,768]{2,1,0:T(8,128)(2,1)S(1)}, bf16[8,48,768]{2,1,0:T(8,128)(2,1)S(1)}, u32[]{:S(2)}, u32[]{:S(2)}) collective-permute-start(bf16[8,48,768]{2,1,0:T(8,128)(2,1)S(1)} %pad_maximum_fusion.1.rest_0_), channel_id=1, source_target_pairs={{0,12},{4,8},{8,4},{12,0},{32,36},{36,32},{40,44},{44,40},{64,76},... | collective-permute-start | bytes 1769480 | tf_op jit(solution)/shard_map/ppermute | solution.py:558
  37.2 3.0 %collective-permute-start.12 = (bf16[8,48,768]{2,1,0:T(8,128)(2,1)S(1)}, bf16[8,48,768]{2,1,0:T(8,128)(2,1)S(1)}, u32[]{:S(2)}, u32[]{:S(2)}) collective-permute-start(bf16[8,48,768]{2,1,0:T(8,128)(2,1)S(1)} %pad_maximum_fusion.4.rest_4_), channel_id=1, source_target_pairs={{0,3},{1,2},{2,1},{3,0},{32,33},{33,32},{34,35},{35,34},{64,67},{6... | collective-permute-start | bytes 1769480 | tf_op jit(solution)/shard_map/ppermute | solution.py:558
  40.8 8.4 %shard_map.102 = (bf16[512,1536]{1,0:T(8,128)(2,1)}, bf16[512,1536]{1,0:T(8,128)(2,1)}, f32[512,128]{1,0:T(8,128)}, bf16[1536,512]{1,0:T(8,128)(2,1)}) custom-call(s32[2]{0:T(128)} %bitcast.54, bf16[2,512,1536]{2,1,0:T(8,128)(2,1)} %bitcast.57, f32[8,1536]{1,0:T(8,128)} %maximum_convert_fusion.taps.rest_14_), custom_call_target="tpu_custom_call" | custom-call | flops 8000000000 | bytes 1048576 | tf_op jit(solution)/shard_map/pallas_call | solution.py:149
  49.3 3.7 %collective-permute-done.9.rest_5_ = bf16[8,48,768]{2,1,0:T(8,128)(2,1)S(1)} collective-permute-done((bf16[8,48,768]{2,1,0:T(8,128)(2,1)S(1)}, bf16[8,48,768]{2,1,0:T(8,128)(2,1)S(1)}, u32[]{:S(2)}, u32[]{:S(2)}) %collective-permute-start.9) | collective-permute-done | bytes 589856 | tf_op jit(solution)/shard_map/ppermute | solution.py:558
  53.0 8.5 %shard_map.103 = (bf16[512,1536]{1,0:T(8,128)(2,1)}, bf16[512,1536]{1,0:T(8,128)(2,1)}, f32[512,128]{1,0:T(8,128)}, bf16[1536,512]{1,0:T(8,128)(2,1)}) custom-call(s32[2]{0:T(128)} %bitcast.55, bf16[2,512,1536]{2,1,0:T(8,128)(2,1)} %bitcast.58, f32[8,1536]{1,0:T(8,128)} %maximum_convert_fusion.taps.rest_14_), custom_call_target="tpu_custom_call" | custom-call | flops 8000000000 | bytes 1048576 | tf_op jit(solution)/shard_map/pallas_call | solution.py:149
  61.6 2.5 %collective-permute-done.11.rest_3_ = bf16[8,48,768]{2,1,0:T(8,128)(2,1)S(1)} collective-permute-done((bf16[8,48,768]{2,1,0:T(8,128)(2,1)S(1)}, bf16[8,48,768]{2,1,0:T(8,128)(2,1)S(1)}, u32[]{:S(2)}, u32[]{:S(2)}) %collective-permute-start.11) | collective-permute-done | bytes 589856 | tf_op jit(solution)/shard_map/ppermute | solution.py:558
  78.0 44.9 %collective-permute-done.17.come.rest_1_ = bf16[512,1536]{1,0:T(8,128)(2,1)S(1)} collective-permute-done((bf16[512,1536]{1,0:T(8,128)(2,1)}, bf16[512,1536]{1,0:T(8,128)(2,1)S(1)}, u32[]{:S(2)}, u32[]{:S(2)}) %collective-permute-start.17) | collective-permute-done | bytes 1572896 | tf_op jit(solution)/shard_map/ppermute | solution.py:640
  124.1 10.3 %shard_map.109 = (bf16[512,1536]{1,0:T(8,128)(2,1)}, bf16[2,512,1536]{2,1,0:T(8,128)(2,1)}, f32[2,8,1536]{2,1,0:T(8,128)}) custom-call(s32[136]{0:T(256)} %concatenate.51.meta, bf16[2,512,1536]{2,1,0:T(8,128)(2,1)} %bitcast.42, bf16[512,1536]{1,0:T(8,128)(2,1)} %copy-done.11, ...), custom_call_target="tpu_custom_call", output_to_operand_aliasing={{1}: (19, {}), {2}: (20, {})} | custom-call | flops 1000000000 | bytes 1048576 | tf_op jit(solution)/shard_map/pallas_call | solution.py:342
  135.9 5.1 %shard_map.110 = f32[8,1536]{1,0:T(8,128)} custom-call(s32[136]{0:T(256)} %concatenate.51.meta, bf16[2,512,1536]{2,1,0:T(8,128)(2,1)} %bitcast.59, bf16[2,512,1536]{2,1,0:T(8,128)(2,1)} %get-tuple-element.86.mixed_in.rest_15_, f32[2,8,1536]{2,1,0:T(8,128)} %get-tuple-element.87.gain_in.rest_16_, f32[8,1536]{1,0:T(8,128)} %maximum_convert_fusion.taps.rest_14_), custom_call_target="tpu_custom_call" | custom-call | flops 5000000000 | bytes 1048576 | tf_op jit(solution)/shard_map/pallas_call | solution.py:514
  142.1 11.3 %shard_map.113 = (bf16[16,48,768]{2,1,0:T(8,128)(2,1)}, bf16[16,48,768]{2,1,0:T(8,128)(2,1)}, bf16[16,48,768]{2,1,0:T(8,128)(2,1)}, bf16[16,48,768]{2,1,0:T(8,128)(2,1)}) custom-call(s32[136]{0:T(256)} %concatenate.51.meta, bf16[1536,512]{1,0:T(8,128)(2,1)} %get-tuple-element.93.act_a, bf16[1536,512]{1,0:T(8,128)(2,1)} %get-tuple-element.94.act_b, ...), custom_call_target="tpu_custom_call" | custom-call | flops 8000000000 | bytes 1048576 | tf_op jit(solution)/shard_map/pallas_call | solution.py:424
  155.7 10.3 %shard_map.111 = (bf16[512,1536]{1,0:T(8,128)(2,1)}, bf16[2,512,1536]{2,1,0:T(8,128)(2,1)}, f32[2,8,1536]{2,1,0:T(8,128)}) custom-call(s32[136]{0:T(256)} %concatenate.51.meta, bf16[2,512,1536]{2,1,0:T(8,128)(2,1)} %bitcast.44, bf16[512,1536]{1,0:T(8,128)(2,1)} %copy-done.10, ...), custom_call_target="tpu_custom_call", output_to_operand_aliasing={{1}: (19, {}), {2}: (20, {})} | custom-call | flops 1000000000 | bytes 1048576 | tf_op jit(solution)/shard_map/pallas_call | solution.py:342
  166.1 6.2 %shard_map.112 = (f32[8,1536]{1,0:T(8,128)}, bf16[2,512,1536]{2,1,0:T(8,128)(2,1)}) custom-call(s32[136]{0:T(256)} %concatenate.51.meta, bf16[2,512,1536]{2,1,0:T(8,128)(2,1)} %bitcast.60, bf16[2,512,1536]{2,1,0:T(8,128)(2,1)} %get-tuple-element.89.mixed_in, f32[2,8,1536]{2,1,0:T(8,128)} %get-tuple-element.90.gain_in, ...), custom_call_target="tpu_custom_call" | custom-call | flops 5000000000 | bytes 1048576 | tf_op jit(solution)/shard_map/pallas_call | solution.py:514
  175.3 2.7 %collective-permute-start.24 = (bf16[8,48,768]{2,1,0:T(8,128)(2,1)S(1)}, bf16[8,48,768]{2,1,0:T(8,128)(2,1)S(1)}, u32[]{:S(2)}, u32[]{:S(2)}) collective-permute-start(bf16[8,48,768]{2,1,0:T(8,128)(2,1)S(1)} %slice.194), channel_id=1, source_target_pairs={{0,12},{4,8},{8,4},{12,0},{32,36},{36,32},{40,44},{44,40},{64,76},... | collective-permute-start | bytes 1769480 | tf_op jit(solution)/shard_map/ppermute | solution.py:558
  179.8 4.7 %collective-permute-done.22 = f32[16,768]{1,0:T(8,128)S(1)} collective-permute-done((f32[16,768]{1,0:T(8,128)S(1)}, f32[16,768]{1,0:T(8,128)S(1)}, u32[]{:S(2)}, u32[]{:S(2)}) %collective-permute-start.22) | collective-permute-done | bytes 49184 | tf_op jit(solution)/shard_map/ppermute | solution.py:558
  185.1 4.7 %collective-permute-done.23 = f32[16,768]{1,0:T(8,128)S(1)} collective-permute-done((f32[16,768]{1,0:T(8,128)S(1)}, f32[16,768]{1,0:T(8,128)S(1)}, u32[]{:S(2)}, u32[]{:S(2)}) %collective-permute-start.23) | collective-permute-done | bytes 49184 | tf_op jit(solution)/shard_map/ppermute | solution.py:558
  191.2 5.6 %collective-permute-done.29 = bf16[4,48,768]{2,1,0:T(8,128)(2,1)S(1)} collective-permute-done((bf16[4,48,768]{2,1,0:T(8,128)(2,1)S(1)}, bf16[4,48,768]{2,1,0:T(8,128)(2,1)S(1)}, u32[]{:S(2)}, u32[]{:S(2)}) %collective-permute-start.29) | collective-permute-done | bytes 294944 | tf_op jit(solution)/shard_map/ppermute | solution.py:558
  199.8 3.5 %collective-permute-done.30 = bf16[2,48,768]{2,1,0:T(8,128)(2,1)S(1)} collective-permute-done((bf16[2,48,768]{2,1,0:T(8,128)(2,1)S(1)}, bf16[2,48,768]{2,1,0:T(8,128)(2,1)S(1)}, u32[]{:S(2)}, u32[]{:S(2)}) %collective-permute-start.30) | collective-permute-done | bytes 147488 | tf_op jit(solution)/shard_map/ppermute | solution.py:558
  203.4 3.1 %collective-permute-start.31 = (bf16[48,768]{1,0:T(8,128)(2,1)S(1)}, bf16[48,768]{1,0:T(8,128)(2,1)S(1)}, u32[]{:S(2)}, u32[]{:S(2)}) collective-permute-start(bf16[48,768]{1,0:T(8,128)(2,1)S(1)} %fusion.7), channel_id=1, source_target_pairs={{0,16},{16,0},{1,17},{17,1},{2,18},{18,2},{3,19},{19,3},{4,20},{20... | collective-permute-start | bytes 221192 | tf_op jit(solution)/shard_map/ppermute | solution.py:548
  209.3 3.4 %collective-permute-done.28 = bf16[64,768]{1,0:T(8,128)(2,1)S(1)} collective-permute-done((bf16[64,768]{1,0:T(8,128)(2,1)S(1)}, bf16[64,768]{1,0:T(8,128)(2,1)S(1)}, u32[]{:S(2)}, u32[]{:S(2)}) %collective-permute-start.28) | collective-permute-done | bytes 98336 | tf_op jit(solution)/shard_map/ppermute | solution.py:548
  (136 shorter events, 50.9 us)
Async XLA Ops:
  2.5 6.2 %collective-permute-start = (bf16[64,768]{1,0:T(8,128)(2,1)S(1)}, bf16[64,768]{1,0:T(8,128)(2,1)S(1)}, u32[]{:S(2)}, u32[]{:S(2)}) collective-permute-start(bf16[64,768]{1,0:T(8,128)(2,1)S(1)} %get-tuple-element.120), channel_id=1, source_target_pairs={{0,16},{16,0},{1,17},{17,1},{2,18},{18,2},{3,19},{19,3},{4,20},{20... | collective-permute-start | bytes 294920 | tf_op jit(solution)/shard_map/ppermute | solution.py:548
  5.7 5.9 %collective-permute-start.5 = (bf16[48,768]{1,0:T(8,128)(2,1)S(1)}, bf16[48,768]{1,0:T(8,128)(2,1)S(1)}, u32[]{:S(2)}, u32[]{:S(2)}) collective-permute-start(bf16[48,768]{1,0:T(8,128)(2,1)S(1)} %get-tuple-element.117), channel_id=1, source_target_pairs={{0,16},{16,0},{1,17},{17,1},{2,18},{18,2},{3,19},{19,3},{4,20},{20... | collective-permute-start | bytes 221192 | tf_op jit(solution)/shard_map/ppermute | solution.py:548
  11.6 6.2 %collective-permute-start.6 = (bf16[2,48,768]{2,1,0:T(8,128)(2,1)S(1)}, bf16[2,48,768]{2,1,0:T(8,128)(2,1)S(1)}, u32[]{:S(2)}, u32[]{:S(2)}) collective-permute-start(bf16[2,48,768]{2,1,0:T(8,128)(2,1)S(1)} %pad_maximum_fusion.8), channel_id=1, source_target_pairs={{0,4},{4,0},{8,12},{12,8},{32,44},{36,40},{40,36},{44,32},{64,68},... | collective-permute-start | bytes 442376 | tf_op jit(solution)/shard_map/ppermute | solution.py:558
  14.5 9.1 %collective-permute-start.2 = (bf16[4,64,768]{2,1,0:T(8,128)(2,1)S(1)}, bf16[4,64,768]{2,1,0:T(8,128)(2,1)S(1)}, u32[]{:S(2)}, u32[]{:S(2)}) collective-permute-start(bf16[4,64,768]{2,1,0:T(8,128)(2,1)S(1)} %pad_maximum_fusion.5), channel_id=1, source_target_pairs={{0,3},{1,2},{2,1},{3,0},{32,33},{33,32},{34,35},{35,34},{64,67},{6... | collective-permute-start | bytes 1179656 | tf_op jit(solution)/shard_map/ppermute | solution.py:558
  17.8 9.1 %collective-permute-start.7 = (bf16[4,48,768]{2,1,0:T(8,128)(2,1)S(1)}, bf16[4,48,768]{2,1,0:T(8,128)(2,1)S(1)}, u32[]{:S(2)}, u32[]{:S(2)}) collective-permute-start(bf16[4,48,768]{2,1,0:T(8,128)(2,1)S(1)} %pad_maximum_fusion.6), channel_id=1, source_target_pairs={{0,12},{4,8},{8,4},{12,0},{32,36},{36,32},{40,44},{44,40},{64,76},... | collective-permute-start | bytes 884744 | tf_op jit(solution)/shard_map/ppermute | solution.py:558
  27.6 6.3 %collective-permute-start.4 = (bf16[16,768]{1,0:T(8,128)(2,1)S(1)}, bf16[16,768]{1,0:T(8,128)(2,1)S(1)}, u32[]{:S(2)}, u32[]{:S(2)}) collective-permute-start(bf16[16,768]{1,0:T(8,128)(2,1)S(1)} %add.82), channel_id=1, source_target_pairs={{0,12},{4,8},{8,4},{12,0},{32,36},{36,32},{40,44},{44,40},{64,76},... | collective-permute-start | bytes 73736 | tf_op jit(solution)/shard_map/ppermute | solution.py:558
  33.9 27.7 %collective-permute-start.10 = (bf16[8,48,768]{2,1,0:T(8,128)(2,1)S(1)}, bf16[8,48,768]{2,1,0:T(8,128)(2,1)S(1)}, u32[]{:S(2)}, u32[]{:S(2)}) collective-permute-start(bf16[8,48,768]{2,1,0:T(8,128)(2,1)S(1)} %pad_maximum_fusion.1.rest_0_), channel_id=1, source_target_pairs={{0,12},{4,8},{8,4},{12,0},{32,36},{36,32},{40,44},{44,40},{64,76},... | collective-permute-start | bytes 1769480 | tf_op jit(solution)/shard_map/ppermute | solution.py:558
  37.2 12.1 %collective-permute-start.8 = (bf16[8,48,768]{2,1,0:T(8,128)(2,1)S(1)}, bf16[8,48,768]{2,1,0:T(8,128)(2,1)S(1)}, u32[]{:S(2)}, u32[]{:S(2)}) collective-permute-start(bf16[8,48,768]{2,1,0:T(8,128)(2,1)S(1)} %pad_maximum_fusion.1.rest_0_), channel_id=1, source_target_pairs={{0,4},{4,0},{8,12},{12,8},{32,44},{36,40},{40,36},{44,32},{64,68},... | collective-permute-start | bytes 1769480 | tf_op jit(solution)/shard_map/ppermute | solution.py:558
  37.2 24.4 %collective-permute-start.12 = (bf16[8,48,768]{2,1,0:T(8,128)(2,1)S(1)}, bf16[8,48,768]{2,1,0:T(8,128)(2,1)S(1)}, u32[]{:S(2)}, u32[]{:S(2)}) collective-permute-start(bf16[8,48,768]{2,1,0:T(8,128)(2,1)S(1)} %pad_maximum_fusion.4.rest_4_), channel_id=1, source_target_pairs={{0,3},{1,2},{2,1},{3,0},{32,33},{33,32},{34,35},{35,34},{64,67},{6... | collective-permute-start | bytes 1769480 | tf_op jit(solution)/shard_map/ppermute | solution.py:558
  40.2 12.8 %collective-permute-start.9 = (bf16[8,48,768]{2,1,0:T(8,128)(2,1)S(1)}, bf16[8,48,768]{2,1,0:T(8,128)(2,1)S(1)}, u32[]{:S(2)}, u32[]{:S(2)}) collective-permute-start(bf16[8,48,768]{2,1,0:T(8,128)(2,1)S(1)} %pad_maximum_fusion.4.rest_4_), channel_id=1, source_target_pairs={{0,1},{1,0},{2,3},{3,2},{32,35},{33,34},{34,33},{35,32},{64,65},{6... | collective-permute-start | bytes 1769480 | tf_op jit(solution)/shard_map/ppermute | solution.py:558
  53.0 11.1 %collective-permute-start.11 = (bf16[8,48,768]{2,1,0:T(8,128)(2,1)S(1)}, bf16[8,48,768]{2,1,0:T(8,128)(2,1)S(1)}, u32[]{:S(2)}, u32[]{:S(2)}) collective-permute-start(bf16[8,48,768]{2,1,0:T(8,128)(2,1)S(1)} %collective-permute-done.8.rest_1_), channel_id=1, source_target_pairs={{0,12},{4,8},{8,4},{12,0},{32,36},{36,32},{40,44},{44,40},{64,76},... | collective-permute-start | bytes 1769480 | tf_op jit(solution)/shard_map/ppermute | solution.py:558
  53.0 11.2 %collective-permute-start.13 = (bf16[8,48,768]{2,1,0:T(8,128)(2,1)S(1)}, bf16[8,48,768]{2,1,0:T(8,128)(2,1)}, u32[]{:S(2)}, u32[]{:S(2)}) collective-permute-start(bf16[8,48,768]{2,1,0:T(8,128)(2,1)S(1)} %collective-permute-done.9.rest_5_), channel_id=1, source_target_pairs={{0,3},{1,2},{2,1},{3,0},{32,33},{33,32},{34,35},{35,34},{64,67},{6... | collective-permute-start | bytes 1769480 | tf_op jit(solution)/shard_map/ppermute | solution.py:558
  75.5 47.4 %collective-permute-start.17 = (bf16[512,1536]{1,0:T(8,128)(2,1)}, bf16[512,1536]{1,0:T(8,128)(2,1)S(1)}, u32[]{:S(2)}, u32[]{:S(2)}) collective-permute-start(bf16[512,1536]{1,0:T(8,128)(2,1)} %get-tuple-element.81.rest_3_), channel_id=1, source_target_pairs={{32,0},{33,1},{34,2},{35,3},{36,4},{37,5},{38,6},{39,7},{40,8},{41... | collective-permute-start | bytes 4718600 | tf_op jit(solution)/shard_map/ppermute | solution.py:640
  134.4 6.6 %collective-permute-start.19 = (bf16[512,1536]{1,0:T(8,128)(2,1)}, bf16[512,1536]{1,0:T(8,128)(2,1)S(1)}, u32[]{:S(2)}, u32[]{:S(2)}) collective-permute-start(bf16[512,1536]{1,0:T(8,128)(2,1)} %get-tuple-element.85.rest_4_), channel_id=1, source_target_pairs={{32,0},{33,1},{34,2},{35,3},{36,4},{37,5},{38,6},{39,7},{40,8},{41... | collective-permute-start | bytes 4718600 | tf_op jit(solution)/shard_map/ppermute | solution.py:640
  153.4 19.7 %collective-permute-start.20 = (bf16[16,48,768]{2,1,0:T(8,128)(2,1)}, bf16[16,48,768]{2,1,0:T(8,128)(2,1)S(1)}, u32[]{:S(2)}, u32[]{:S(2)}) collective-permute-start(bf16[16,48,768]{2,1,0:T(8,128)(2,1)} %get-tuple-element.96), channel_id=1, source_target_pairs={{0,4},{4,0},{8,12},{12,8},{32,44},{36,40},{40,36},{44,32},{64,68},... | collective-permute-start | bytes 3538952 | tf_op jit(solution)/shard_map/ppermute | solution.py:558
  155.7 17.4 %collective-permute-start.21 = (bf16[16,48,768]{2,1,0:T(8,128)(2,1)}, bf16[16,48,768]{2,1,0:T(8,128)(2,1)}, u32[]{:S(2)}, u32[]{:S(2)}) collective-permute-start(bf16[16,48,768]{2,1,0:T(8,128)(2,1)} %get-tuple-element.97), channel_id=1, source_target_pairs={{0,1},{1,0},{2,3},{3,2},{32,35},{33,34},{34,33},{35,32},{64,65},{6... | collective-permute-start | bytes 3538952 | tf_op jit(solution)/shard_map/ppermute | solution.py:558
  175.3 14.5 %collective-permute-start.24 = (bf16[8,48,768]{2,1,0:T(8,128)(2,1)S(1)}, bf16[8,48,768]{2,1,0:T(8,128)(2,1)S(1)}, u32[]{:S(2)}, u32[]{:S(2)}) collective-permute-start(bf16[8,48,768]{2,1,0:T(8,128)(2,1)S(1)} %slice.194), channel_id=1, source_target_pairs={{0,12},{4,8},{8,4},{12,0},{32,36},{36,32},{40,44},{44,40},{64,76},... | collective-permute-start | bytes 1769480 | tf_op jit(solution)/shard_map/ppermute | solution.py:558
  178.0 11.8 %collective-permute-start.25 = (bf16[8,48,768]{2,1,0:T(8,128)(2,1)S(1)}, bf16[8,48,768]{2,1,0:T(8,128)(2,1)S(1)}, u32[]{:S(2)}, u32[]{:S(2)}) collective-permute-start(bf16[8,48,768]{2,1,0:T(8,128)(2,1)S(1)} %slice.193), channel_id=1, source_target_pairs={{0,3},{1,2},{2,1},{3,0},{32,33},{33,32},{34,35},{35,34},{64,67},{6... | collective-permute-start | bytes 1769480 | tf_op jit(solution)/shard_map/ppermute | solution.py:558
  190.0 6.8 %collective-permute-start.29 = (bf16[4,48,768]{2,1,0:T(8,128)(2,1)S(1)}, bf16[4,48,768]{2,1,0:T(8,128)(2,1)S(1)}, u32[]{:S(2)}, u32[]{:S(2)}) collective-permute-start(bf16[4,48,768]{2,1,0:T(8,128)(2,1)S(1)} %slice.195), channel_id=1, source_target_pairs={{0,4},{4,0},{8,12},{12,8},{32,44},{36,40},{40,36},{44,32},{64,68},... | collective-permute-start | bytes 884744 | tf_op jit(solution)/shard_map/ppermute | solution.py:558
  190.3 7.9 %collective-permute-start.26 = (bf16[4,64,768]{2,1,0:T(8,128)(2,1)S(1)}, bf16[4,64,768]{2,1,0:T(8,128)(2,1)S(1)}, u32[]{:S(2)}, u32[]{:S(2)}) collective-permute-start(bf16[4,64,768]{2,1,0:T(8,128)(2,1)S(1)} %fusion.2), channel_id=1, source_target_pairs={{0,1},{1,0},{2,3},{3,2},{32,35},{33,34},{34,33},{35,32},{64,65},{6... | collective-permute-start | bytes 1179656 | tf_op jit(solution)/shard_map/ppermute | solution.py:558
  196.9 6.4 %collective-permute-start.30 = (bf16[2,48,768]{2,1,0:T(8,128)(2,1)S(1)}, bf16[2,48,768]{2,1,0:T(8,128)(2,1)S(1)}, u32[]{:S(2)}, u32[]{:S(2)}) collective-permute-start(bf16[2,48,768]{2,1,0:T(8,128)(2,1)S(1)} %slice.197), channel_id=1, source_target_pairs={{0,12},{4,8},{8,4},{12,0},{32,36},{36,32},{40,44},{44,40},{64,76},... | collective-permute-start | bytes 442376 | tf_op jit(solution)/shard_map/ppermute | solution.py:558
  198.3 8.2 %collective-permute-start.27 = (bf16[2,64,768]{2,1,0:T(8,128)(2,1)S(1)}, bf16[2,64,768]{2,1,0:T(8,128)(2,1)S(1)}, u32[]{:S(2)}, u32[]{:S(2)}) collective-permute-start(bf16[2,64,768]{2,1,0:T(8,128)(2,1)S(1)} %slice.196), channel_id=1, source_target_pairs={{0,3},{1,2},{2,1},{3,0},{32,33},{33,32},{34,35},{35,34},{64,67},{6... | collective-permute-start | bytes 589832 | tf_op jit(solution)/shard_map/ppermute | solution.py:558
  203.4 5.9 %collective-permute-start.31 = (bf16[48,768]{1,0:T(8,128)(2,1)S(1)}, bf16[48,768]{1,0:T(8,128)(2,1)S(1)}, u32[]{:S(2)}, u32[]{:S(2)}) collective-permute-start(bf16[48,768]{1,0:T(8,128)(2,1)S(1)} %fusion.7), channel_id=1, source_target_pairs={{0,16},{16,0},{1,17},{17,1},{2,18},{18,2},{3,19},{19,3},{4,20},{20... | collective-permute-start | bytes 221192 | tf_op jit(solution)/shard_map/ppermute | solution.py:548
  206.5 6.2 %collective-permute-start.28 = (bf16[64,768]{1,0:T(8,128)(2,1)S(1)}, bf16[64,768]{1,0:T(8,128)(2,1)S(1)}, u32[]{:S(2)}, u32[]{:S(2)}) collective-permute-start(bf16[64,768]{1,0:T(8,128)(2,1)S(1)} %fusion.6), channel_id=1, source_target_pairs={{0,16},{16,0},{1,17},{17,1},{2,18},{18,2},{3,19},{19,3},{4,20},{20... | collective-permute-start | bytes 294920 | tf_op jit(solution)/shard_map/ppermute | solution.py:548
  (25 other events, 146.1 us)
